TPU v7x, 128 devices: a whole 4x4x4 slice. The times are simulated.
128 devices in a mesh: wide: 16 (over x, y_hi, core), narrow: 8 (over z, y_lo).
Axes of the slice: x: 4, y: 4 (y_hi: 2, y_lo: 2; y = y_hi * 2 + y_lo), z: 4, core: 2. Of those that a mesh axis runs over, the one named last changes fastest.
Arguments:
- tokens: bfloat16 [65536, 768], P(('wide', 'narrow')), may hold values from -6 to 6
- seq_lengths: int32 [128, 2], P(('wide', 'narrow')), may hold values from 1 to 384, 512 in all within a row
- key_mask: int32 [65536], P(('wide', 'narrow')), may hold values 0 or 1
- routes: int32 [65536, 2], P(('wide', 'narrow')), may hold values from 0 to 15, all different within a row
- cotangent: bfloat16 [65536, 768], P(('wide', 'narrow')), may hold values from -6 to 6
- qkv_weight: float32 [768, 2304], P(('wide', 'narrow')), may hold values from -0.21875 to 0.21875
- out_weight: float32 [768, 768], P(('wide', 'narrow')), may hold values from -0.875 to 0.875
- router_weight: float32 [768, 16], P(('wide', 'narrow')), may hold values from -0.15625 to 0.15625
- norm_gains: float32 [2, 768], P(None, ('wide', 'narrow')), may hold values from 0.5 to 1.5
- norm_biases: float32 [2, 768], P(None, ('wide', 'narrow')), may hold values from -1.8 to 1.8
- up_train: float32 [8, 768, 3072], P('narrow', 'wide'), may hold values from -0.21875 to 0.21875
- down_train: float32 [8, 3072, 768], P('narrow', 'wide'), may hold values from -0.109375 to 0.109375
- up_frozen: bfloat16 [8, 768, 3072], P('narrow', 'wide'), may hold values from -0.21875 to 0.21875
- down_frozen: bfloat16 [8, 3072, 768], P('narrow', 'wide'), may hold values from -0.109375 to 0.109375
Outputs:
- block_out: bfloat16 [65536, 768], P(('wide', 'narrow'))
- input_grad: float32 [65536, 768], P(('wide', 'narrow'))
- grad_qkv: float32 [768, 2304], P(('wide', 'narrow'))
- grad_out: float32 [768, 768], P(('wide', 'narrow'))
- grad_router: float32 [768, 16], P(('wide', 'narrow'))
- grad_gains: float32 [2, 768], P(None, ('wide', 'narrow'))
- grad_biases: float32 [2, 768], P(None, ('wide', 'narrow'))
- grad_up: float32 [8, 768, 3072], P('narrow', 'wide')
- grad_down: float32 [8, 3072, 768], P('narrow', 'wide')
Inputs may be any that keep to these rules, and one draw needn't show every extreme that they name: `seq_lengths`: the 2 lengths of a row add up to 512; no length exceeds 384. `routes`: the 2 experts of a token differ.
All inputs are finite; a program needn't handle non-finite values. No bound on the sum of `key_mask` on one device may be relied on, other than what follows from the above.
Results may differ from a plain program's by a relative error of at most 0.015.
Values may be sent and summed in bfloat16 or wider, within the bound.
No kernel may reach another device: no remote copies, remote signals or barrier semaphores. Data moves between devices by JAX's collectives and lax.ppermute only.
A program may use at most 256 MiB of HBM per device.

v0:
```python
import jax
import jax.numpy as jnp
from jax import lax
from jax.sharding import PartitionSpec as P

HEAD = 64
TOP = 2


def rows_first(arrays, axis, dims):
    turned = [jnp.moveaxis(a, dim, 0) for a, dim in zip(arrays, dims)]
    widths = [t[0].size for t in turned]
    both = jnp.concatenate([t.reshape(-1, w) for t, w in zip(turned, widths)], axis=1)
    result = lax.all_gather(both, axis, axis=0, tiled=True)
    pieces = jnp.split(result, [sum(widths[:k]) for k in range(1, len(widths))], axis=1)
    return tuple(
        (
            jnp.moveaxis(b.reshape(-1, *t.shape[1:]), 0, dim)
            for b, t, dim in zip(pieces, turned, dims)
        )
    )


def laid_out(pieces, dim):
    dims = list(pieces.shape[1:])
    dims[dim] *= pieces.shape[0]
    return jnp.moveaxis(pieces, 0, dim).reshape(dims)


def gather_together(arrays, axis, dims):
    ravelled = jnp.concatenate([a.reshape(-1) for a in arrays])
    lines, at, gathered = (lax.all_gather(ravelled, axis), 0, [])
    for a, dim in zip(arrays, dims):
        pieces = lines[:, at : at + a.size].reshape(-1, *a.shape)
        gathered.append(laid_out(pieces, dim))
        at += a.size
    return tuple(gathered)


def in_blocks(x, dim, peers):
    dims = x.shape
    pieces = x.reshape(*dims[:dim], peers, dims[dim] // peers, *dims[dim + 1 :])
    return jnp.moveaxis(pieces, dim, 0)


def one_scatter(arrays, axis, dims):
    peers = lax.axis_size(axis)
    pieces = [in_blocks(a, dim, peers) for a, dim in zip(arrays, dims)]
    lines = jnp.concatenate([b.reshape(peers, -1) for b in pieces], axis=1)
    extent = max(16, -(-lines.shape[1] // 1024) * 8)
    lines = jnp.pad(lines, ((0, 0), (0, extent * 128 - lines.shape[1]))).reshape(-1, 128)
    ravelled, at, gathered = (lax.psum_scatter(lines, axis, tiled=True).reshape(-1), 0, [])
    for b in pieces:
        part = b[0]
        gathered.append(ravelled[at : at + part.size].reshape(part.shape))
        at += part.size
    return tuple(gathered)


def layer_norm(values, gain_row, bias_row):
    average = jnp.mean(values, -1, keepdims=True)
    centered = values - average
    variance = jnp.mean(centered * centered, -1, keepdims=True)
    return centered * lax.rsqrt(variance + 1e-05) * gain_row + bias_row


def smooth_act(pre_act):
    return jax.nn.gelu(pre_act, approximate=True)


def visible(lengths_row, mask_row, count):
    places = lax.iota(jnp.int32, count)
    seq_ends = jnp.cumsum(lengths_row)
    segment = jnp.sum((places[:, None] >= seq_ends[None, :]).astype(jnp.int32), 1)
    same_seq = segment[:, None] == segment[None, :]
    causal = places[None, :] <= places[:, None]
    open_key = (mask_row[None, :] == 1) | (places[:, None] == places[None, :])
    return same_seq & causal & open_key


def masked_scores(q_part, k_part, allowed):
    scores = jnp.einsum("qhd,khd->hqk", q_part, k_part, preferred_element_type=jnp.float32) * 0.125
    return jnp.where(allowed[None], scores, -1e30)


def shards(
    tokens,
    seq_lengths,
    key_mask,
    routes,
    cotangent,
    qkv_weight,
    out_weight,
    router_weight,
    norm_gains,
    norm_biases,
    up_train,
    down_train,
    up_frozen,
    down_frozen,
):
    row_count, width = tokens.shape
    head_count = width // HEAD
    groups = lax.axis_size("narrow")
    experts = 2 * groups
    capacity = 3 * row_count // experts
    pair_count = TOP * row_count
    slot_count = experts * capacity
    w_qkv, w_out, w_router, gains, biases = rows_first(
        (
            qkv_weight.astype(jnp.bfloat16),
            out_weight.astype(jnp.bfloat16),
            router_weight.astype(jnp.bfloat16),
            norm_gains.astype(jnp.bfloat16),
            norm_biases.astype(jnp.bfloat16),
        ),
        ("wide", "narrow"),
        (0, 0, 0, 1, 1),
    )
    up_mine, down_mine, up_fixed, down_fixed = gather_together(
        (up_train.astype(jnp.bfloat16), down_train.astype(jnp.bfloat16), up_frozen, down_frozen),
        "wide",
        (1, 1, 1, 1),
    )
    up_all = jnp.concatenate((up_mine, up_fixed), 0)
    down_all = jnp.concatenate((down_mine, down_fixed), 0)
    allowed = visible(seq_lengths[0], key_mask, row_count)
    x_in = tokens.astype(jnp.float32)
    gain_one = gains[0].astype(jnp.float32)
    bias_one = biases[0].astype(jnp.float32)
    h_one = layer_norm(x_in, gain_one, bias_one).astype(jnp.bfloat16)
    qkv_all = jnp.dot(h_one, w_qkv, preferred_element_type=jnp.float32).astype(jnp.bfloat16)
    q_part = qkv_all[:, :width].reshape(row_count, head_count, HEAD)
    k_part = qkv_all[:, width : 2 * width].reshape(row_count, head_count, HEAD)
    v_part = qkv_all[:, 2 * width :].reshape(row_count, head_count, HEAD)
    scores = masked_scores(q_part, k_part, allowed)
    row_peak = jnp.max(scores, -1, keepdims=True)
    exp_scores = jnp.exp(scores - row_peak)
    row_total = jnp.sum(exp_scores, -1, keepdims=True)
    log_total = row_peak + jnp.log(row_total)
    attn_probs = (exp_scores / row_total).astype(jnp.bfloat16)
    attn_out = (
        jnp.einsum("hqk,khd->qhd", attn_probs, v_part, preferred_element_type=jnp.float32)
        .reshape(row_count, width)
        .astype(jnp.bfloat16)
    )
    x_mid = x_in + jnp.dot(attn_out, w_out, preferred_element_type=jnp.float32)
    gain_two = gains[1].astype(jnp.float32)
    bias_two = biases[1].astype(jnp.float32)
    h_two = layer_norm(x_mid, gain_two, bias_two).astype(jnp.bfloat16)
    logits = jnp.dot(h_two, w_router, preferred_element_type=jnp.float32)
    route_hot = routes[:, :, None] == lax.iota(jnp.int32, experts)[None, None, :]
    chosen = jnp.sum(jnp.where(route_hot, logits[:, None, :], 0.0), -1)
    gate_vals = jax.nn.softmax(chosen, -1)
    flat_hot = route_hot.reshape(pair_count, experts).astype(jnp.int32)
    slot_pos = jnp.sum((jnp.cumsum(flat_hot, 0) - flat_hot) * flat_hot, 1)
    is_kept = slot_pos < capacity
    slot_id = jnp.where(is_kept, routes.reshape(-1) * capacity + slot_pos, slot_count)
    slot_owner = (
        jnp.full((slot_count + 1,), pair_count, jnp.int32)
        .at[slot_id]
        .set(lax.iota(jnp.int32, pair_count))[:slot_count]
    )
    filled = slot_owner < pair_count
    pair_src = jnp.minimum(slot_owner, pair_count - 1)
    slot_rows = jnp.where(filled[:, None], h_two[pair_src // TOP], jnp.zeros((), jnp.bfloat16))
    arrived = lax.all_to_all(
        slot_rows.reshape(2, groups, capacity, width),
        "narrow",
        split_axis=1,
        concat_axis=1,
        tiled=True,
    )
    recv_rows = arrived.reshape(2, groups * capacity, width)
    up_vals = jnp.einsum("krd,kdf->krf", recv_rows, up_all, preferred_element_type=jnp.float32)
    activated = smooth_act(up_vals).astype(jnp.bfloat16)
    expert_out = jnp.einsum(
        "krf,kfd->krd", activated, down_all, preferred_element_type=jnp.float32
    ).astype(jnp.bfloat16)
    returned = lax.all_to_all(
        expert_out.reshape(2, groups, capacity, width),
        "narrow",
        split_axis=1,
        concat_axis=1,
        tiled=True,
    )
    pick_index = jnp.minimum(slot_id, slot_count - 1)
    pair_vals = jnp.where(
        is_kept[:, None],
        returned.reshape(slot_count, width)[pick_index],
        jnp.zeros((), jnp.bfloat16),
    )
    pair_vals = pair_vals.astype(jnp.float32).reshape(row_count, TOP, width)
    block_out = (x_mid + jnp.sum(gate_vals[:, :, None] * pair_vals, 1)).astype(jnp.bfloat16)
    w_qkv_b, w_out_b, w_router_b, gains_b, biases_b = (w_qkv, w_out, w_router, gains, biases)
    up_all_b, down_all_b = (up_all, down_all)
    d_res = cotangent.astype(jnp.float32)
    d_gates = jnp.sum(pair_vals * d_res[:, None, :], -1)
    d_chosen = gate_vals * (d_gates - jnp.sum(gate_vals * d_gates, -1, keepdims=True))
    d_logits = jnp.sum(jnp.where(route_hot, d_chosen[:, :, None], 0.0), 1)
    d_pairs = (gate_vals[:, :, None] * d_res[:, None, :]).reshape(pair_count, width)
    d_slot_out = jnp.where(filled[:, None], d_pairs[pair_src], 0.0).astype(jnp.bfloat16)
    d_arrived = lax.all_to_all(
        d_slot_out.reshape(2, groups, capacity, width),
        "narrow",
        split_axis=1,
        concat_axis=1,
        tiled=True,
    )
    d_rows_out = d_arrived.reshape(2, groups * capacity, width)
    d_acts = jnp.einsum("krd,kfd->krf", d_rows_out, down_all_b, preferred_element_type=jnp.float32)
    unused_act, gelu_pull = jax.vjp(smooth_act, up_vals)
    d_up = gelu_pull(d_acts)[0].astype(jnp.bfloat16)
    grad_down_t = jnp.einsum(
        "rf,rd->fd", activated[0], d_rows_out[0], preferred_element_type=jnp.float32
    )
    grad_up_t = jnp.einsum("rd,rf->df", recv_rows[0], d_up[0], preferred_element_type=jnp.float32)
    d_rows = jnp.einsum("krf,kdf->krd", d_up, up_all_b, preferred_element_type=jnp.float32).astype(
        jnp.bfloat16
    )
    d_back = lax.all_to_all(
        d_rows.reshape(2, groups, capacity, width),
        "narrow",
        split_axis=1,
        concat_axis=1,
        tiled=True,
    )
    d_slot_in = jnp.where(
        is_kept[:, None], d_back.reshape(slot_count, width)[pick_index], jnp.zeros((), jnp.bfloat16)
    )
    router_f = w_router_b.astype(jnp.float32)
    d_h_two = jnp.sum(d_slot_in.astype(jnp.float32).reshape(row_count, TOP, width), 1)
    d_h_two = d_h_two + jnp.einsum("re,de->rd", d_logits, router_f)
    grad_router_l = jnp.einsum("rd,re->de", h_two.astype(jnp.float32), d_logits)
    unused_two, pull_two = jax.vjp(
        layer_norm, x_mid, gains_b[1].astype(jnp.float32), biases_b[1].astype(jnp.float32)
    )
    d_mid_norm, d_gain_two, d_bias_two = pull_two(d_h_two)
    d_x_mid = d_res + d_mid_norm
    d_proj = d_x_mid.astype(jnp.bfloat16)
    grad_out_l = jnp.einsum("rd,re->de", attn_out, d_proj, preferred_element_type=jnp.float32)
    d_attn = jnp.einsum("re,de->rd", d_proj, w_out_b, preferred_element_type=jnp.float32).astype(
        jnp.bfloat16
    )
    d_attn_h = d_attn.reshape(row_count, head_count, HEAD)
    probs_back = jnp.exp(masked_scores(q_part, k_part, allowed) - log_total)
    d_probs = jnp.einsum("qhd,khd->hqk", d_attn_h, v_part, preferred_element_type=jnp.float32)
    d_vals = jnp.einsum(
        "hqk,qhd->khd",
        probs_back.astype(jnp.bfloat16),
        d_attn_h,
        preferred_element_type=jnp.float32,
    )
    row_delta = jnp.sum(probs_back * d_probs, -1, keepdims=True)
    d_scores = (probs_back * (d_probs - row_delta)).astype(jnp.bfloat16)
    d_query = (
        jnp.einsum("hqk,khd->qhd", d_scores, k_part, preferred_element_type=jnp.float32) * 0.125
    )
    d_key = jnp.einsum("hqk,qhd->khd", d_scores, q_part, preferred_element_type=jnp.float32) * 0.125
    d_qkv = jnp.concatenate(
        (
            d_query.reshape(row_count, width),
            d_key.reshape(row_count, width),
            d_vals.reshape(row_count, width),
        ),
        1,
    ).astype(jnp.bfloat16)
    grad_qkv_l = jnp.einsum("rd,re->de", h_one, d_qkv, preferred_element_type=jnp.float32)
    d_h_one = jnp.einsum("re,de->rd", d_qkv, w_qkv_b, preferred_element_type=jnp.float32)
    unused_one, pull_one = jax.vjp(
        layer_norm, x_in, gains_b[0].astype(jnp.float32), biases_b[0].astype(jnp.float32)
    )
    d_in_norm, d_gain_one, d_bias_one = pull_one(d_h_one)
    input_grad = d_x_mid + d_in_norm
    grad_gains_l = jnp.stack((d_gain_one, d_gain_two), 0)
    grad_biases_l = jnp.stack((d_bias_one, d_bias_two), 0)
    grad_qkv, grad_out, grad_router, grad_gains, grad_biases = one_scatter(
        (grad_qkv_l, grad_out_l, grad_router_l, grad_gains_l, grad_biases_l),
        ("wide", "narrow"),
        (0, 0, 0, 1, 1),
    )
    grad_up, grad_down = tuple(
        (
            part.astype(jnp.float32)
            for part in one_scatter(
                (grad_up_t[None].astype(jnp.bfloat16), grad_down_t[None].astype(jnp.bfloat16)),
                "wide",
                (1, 1),
            )
        )
    )
    return (
        block_out,
        input_grad,
        grad_qkv,
        grad_out,
        grad_router,
        grad_gains,
        grad_biases,
        grad_up,
        grad_down,
    )


def solution(mesh):
    placed = (
        P(("wide", "narrow"), None),
        P(("wide", "narrow"), None),
        P(("wide", "narrow")),
        P(("wide", "narrow"), None),
        P(("wide", "narrow"), None),
        P(("wide", "narrow"), None),
        P(("wide", "narrow"), None),
        P(("wide", "narrow"), None),
        P(None, ("wide", "narrow")),
        P(None, ("wide", "narrow")),
        P("narrow", "wide", None),
        P("narrow", "wide", None),
        P("narrow", "wide", None),
        P("narrow", "wide", None),
    )
    return jax.shard_map(
        shards,
        mesh=mesh,
        in_specs=placed,
        out_specs=(
            P(("wide", "narrow"), None),
            P(("wide", "narrow"), None),
            P(("wide", "narrow"), None),
            P(("wide", "narrow"), None),
            P(("wide", "narrow"), None),
            P(None, ("wide", "narrow")),
            P(None, ("wide", "narrow")),
            P("narrow", "wide", None),
            P("narrow", "wide", None),
        ),
        check_vma=False,
    )
```

profile of v0, /device:TPU:0, one launch (start us, length us, event | category | flops | bytes accessed | tf_op | source)
XLA Modules:
  0.0 1148.9 jit_solution(2095921612294881925)
XLA Ops:
  27.6 295.2 %all-gather.7.cloned.1.call-done = bf16[128,6,3092]{2,1,0:T(8,128)(2,1)} async-done(((bf16[1,6,3092]{2,1,0:T(8,128)(2,1)}), bf16[128,6,3092]{2,1,0:T(8,128)(2,1)}) %all-gather.7.cloned.1.call-update) | async-done | bytes 4749328 | tf_op jit(solution)/shard_map/all_gather | solution.py:14
  322.8 10.0 reshape.622
  362.7 58.7 %all_to_all.20 = bf16[2,8,96,768]{3,2,0,1:T(8,128)(2,1)S(1)} all-to-all(bf16[2,8,96,768]{3,2,0,1:T(8,128)(2,1)S(1)} %copy_select_fusion.1), channel_id=1, replica_groups=mesh['wide'=16,'narrow'=8] {'narrow'}, dimensions={1} | all-to-all | bytes 4718592 | tf_op jit(solution)/shard_map/all_to_all | solution.py:167
  423.1 46.1 %all-gather.5.cloned.1.call-done = bf16[9437184]{0:T(1024)(128)(2,1)} async-done(((bf16[589824]{0:T(1024)(128)(2,1)}), bf16[9437184]{0:T(1024)(128)(2,1)}) %all-gather.5.cloned.1.call-update) | async-done | bytes 18874384 | tf_op jit(solution)/shard_map/all_gather | solution.py:32
  469.2 22.6 %reshape.618 = bf16[16,589824]{1,0:T(8,128)(2,1)} reshape(bf16[9437184]{0:T(1024)(128)(2,1)} %all-gather.5.cloned.1.call-done) | data formatting | bytes 37748736 | tf_op jit(solution)/shard_map/all_gather | solution.py:32
  491.8 13.7 %fusion.70 = (bf16[16,147456]{1,0:T(8,128)(2,1)}, bf16[16,147456]{1,0:T(8,128)(2,1)}, bf16[16,147456]{1,0:T(8,128)(2,1)}, bf16[16,147456]{1,0:T(8,128)(2,1)}) fusion(bf16[16,589824]{1,0:T(8,128)(2,1)} %reshape.618), kind=kLoop, calls=%fused_computation.172 | loop fusion | bytes 37748736 | tf_op jit(solution)/shard_map/slice | solution.py:34
  543.7 19.4 %multiply_convert_fusion = (bf16[2,768,3072]{2,1,0:T(8,128)(2,1)}, f32[2,768,3072]{2,1,0:T(8,128)}) fusion(bf16[2,768,768]{2,1,0:T(8,128)(2,1)S(1)} %bitcast.132, bf16[2,768,3072]{2,1,0:T(8,128)(2,1)} %copy-done.22), kind=kOutput, calls=%fused_computation.14 | convolution fusion | flops 7290224640 | bytes 40108032 | tf_op jit(solution)/shard_map/krd,kdf->krf/dot_general | solution.py:175
  563.1 10.0 convolution_convert_fusion.4
  589.0 21.2 %all-to-all-done.1 = bf16[2,8,96,768]{3,2,0,1:T(8,128)(2,1)} async-done(((bf16[2,8,96,768]{3,2,0,1:T(8,128)(2,1)}), bf16[2,8,96,768]{3,2,0,1:T(8,128)(2,1)}, u32[]{:S(2)}, u32[]{:S(2)}) %all-to-all-start.1) | async-done | bytes 2359328 | tf_op jit(solution)/shard_map/all_to_all | solution.py:180
  637.8 27.8 %all-to-all-done.2 = bf16[2,8,96,768]{3,2,0,1:T(8,128)(2,1)S(1)} async-done(((bf16[2,8,96,768]{3,2,0,1:T(8,128)(2,1)}), bf16[2,8,96,768]{3,2,0,1:T(8,128)(2,1)S(1)}, u32[]{:S(2)}, u32[]{:S(2)}) %all-to-all-start.2) | async-done | bytes 2359328 | tf_op jit(solution)/shard_map/all_to_all | solution.py:203
  667.3 24.6 %fusion.6 = bf16[2,768,3072]{2,1,0:T(8,128)(2,1)} fusion(f32[2,768,3072]{2,1,0:T(8,128)} %get-tuple-element.49, bf16[2,768,768]{2,1,0:T(8,128)(2,1)} %bitcast.133, bf16[2,3072,768]{2,1,0:T(8,128)(2,1)} %constant_dynamic-update-slice_fusion.2), kind=kOutput, calls=%fused_computation.13 | convolution fusion | flops 7342129152 | bytes 40108032 | tf_op jit(solution)/shard_map/krd,kfd->krf/dot_general | solution.py:211
  691.9 11.1 convolution_convert_fusion.3
  727.8 8.1 convolution_convert_fusion
  751.9 16.9 %convert_reduce_fusion = (f32[512,768]{1,0:T(8,128)S(1)}, f32[512,768]{1,0:T(8,128)S(1)}) fusion(bf16[512,2,768]{2,1,0:T(2,128)(2,1)S(1)} %gather.27, pred[512,2]{1,0:T(8,128)(4,1)S(1)} %copy-done.28, bf16[512,2,768]{2,1,0:T(2,128)(2,1)S(1)} %copy-done.16, f32[512,2]{1,0:T(8,128)S(1)} %copy-done.21), kind=kLoop, calls=%fused_computation.36 | loop fusion | flops 4718592 | bytes 6296576 | tf_op jit(solution)/shard_map/reduce_sum | solution.py:232
  780.0 8.9 fusion.29
  789.0 9.6 multiply_reduce_fusion
  825.5 8.3 reshape_reshape.9
  833.8 12.4 %concatenate.29 = f32[128,18552]{1,0:T(8,128)} concatenate(f32[128,13824]{1,0:T(8,128)} %reshape_reshape.9, f32[128,4608]{1,0:T(8,128)} %reshape_reshape.10, f32[128,96]{1,0:T(8,128)S(1)} %reshape_reshape.11, f32[128,12]{1,0:T(8,128)S(1)} %copy.204, f32[128,12]{1,0:T(8,128)S(1)} %copy.205), dimensions={1} | concatenate | bytes 18997248 | tf_op jit(solution)/shard_map/concatenate | solution.py:49
  846.2 8.5 pad.4
  854.7 10.3 reshape.565
  865.0 11.7 %pad_maximum_fusion = bf16[16,294912]{1,0:T(8,128)(2,1)} fusion(bf16[16,147456]{1,0:T(8,128)(2,1)} %reshape_transpose_reshape.23, bf16[16,147456]{1,0:T(8,128)(2,1)} %reshape_transpose_reshape.22), kind=kLoop, calls=%fused_computation.23 | loop fusion | flops 18874368 | bytes 18874368 | tf_op jit(solution)/shard_map/concatenate | solution.py:49
  876.7 13.4 %reshape.571 = bf16[36864,128]{1,0:T(8,128)(2,1)} reshape(bf16[16,294912]{1,0:T(8,128)(2,1)} %pad_maximum_fusion) | data formatting | bytes 18874368 | tf_op jit(solution)/shard_map/reshape | solution.py:51
  893.4 135.9 %all-reduce.4.cloned.1.call-done = f32[19456,128]{1,0:T(8,128)} async-done(((f32[19456,128]{1,0:T(8,128)}), f32[19456,128]{1,0:T(8,128)}) %all-reduce.4.cloned.1.call-update) | async-done | bytes 9961488
  1036.1 103.0 %reduce-scatter.2.cloned.1.call-done = bf16[2304,128]{1,0:T(8,128)(2,1)} async-done(((bf16[36864,128]{1,0:T(8,128)(2,1)}), bf16[2304,128]{1,0:T(8,128)(2,1)}) %reduce-scatter.2.cloned.1.call-update) | async-done | bytes 589840 | tf_op jit(solution)/shard_map/reduce_scatter | solution.py:52
  (308 shorter events, 226.2 us)
Async XLA Ops:
  7.2 315.6 %all-gather.7.cloned.1.call-start = ((), (), s32[]{:S(2)}) async-start(), calls=%async_computation.7 | async-start | bytes 6604800 | tf_op jit(solution)/shard_map/all_gather | solution.py:14
  11.9 457.3 %all-gather.5.cloned.1.call-start = ((), (), s32[]{:S(2)}) async-start(), calls=%async_computation.6 | async-start | bytes 20054016 | tf_op jit(solution)/shard_map/all_gather | solution.py:32
  26.9 307.6 %copy-start.38 = (f32[512]{0:T(512)}, f32[512]{0:T(512)S(1)}, u32[]{:S(2)}) copy-start(f32[512]{0:T(512)S(1)} %broadcast_multiply_fusion.3) | copy-start | bytes 6148
  27.3 305.6 %copy-start.44 = (f32[512]{0:T(512)}, f32[512]{0:T(512)S(1)}, u32[]{:S(2)}) copy-start(f32[512]{0:T(512)S(1)} %fusion.27) | copy-start | bytes 6148
  27.3 307.2 %copy-start.42 = (f32[512]{0:T(512)}, f32[512]{0:T(512)S(1)}, u32[]{:S(2)}) copy-start(f32[512]{0:T(512)S(1)} %fusion.56) | copy-start | bytes 6148
  27.6 320.1 %copy-start.14 = (pred[512,512]{0,1:T(8,128)(4,1)}, pred[512,512]{0,1:T(8,128)(4,1)S(1)}, u32[]{:S(2)}) copy-start(pred[512,512]{0,1:T(8,128)(4,1)S(1)} %fusion.34) | copy-start | bytes 786436
  334.5 22.2 %copy-start.29 = (f32[768]{0:T(1024)}, f32[768]{0:T(1024)S(1)}, u32[]{:S(2)}) copy-start(f32[768]{0:T(1024)S(1)} %get-tuple-element.55) | copy-start | bytes 9220
  539.1 24.0 %slice-start.9 = ((s8[9437184]{0:T(1024)(128)(4,1)}), s8[4194304]{0:T(1024)(128)(4,1)S(1)}, s32[]{:S(2)}) async-start(s8[9437184]{0:T(1024)(128)(4,1)} %bitcast.128), calls=%async_computation.18 | async-start | bytes 8388608
  543.7 19.4 %slice-start.10 = ((s8[9437184]{0:T(1024)(128)(4,1)}), s8[4194304]{0:T(1024)(128)(4,1)S(1)}, s32[]{:S(2)}) async-start(s8[9437184]{0:T(1024)(128)(4,1)} %bitcast.128), calls=%async_computation.19 | async-start | bytes 8388608
  543.7 19.4 %slice-start.11 = ((s8[9437184]{0:T(1024)(128)(4,1)}), s8[1048576]{0:T(1024)(128)(4,1)S(1)}, s32[]{:S(2)}) async-start(s8[9437184]{0:T(1024)(128)(4,1)} %bitcast.128), calls=%async_computation.20 | async-start | bytes 2097152
  574.7 35.5 %all-to-all-start.1 = ((bf16[2,8,96,768]{3,2,0,1:T(8,128)(2,1)}), bf16[2,8,96,768]{3,2,0,1:T(8,128)(2,1)}, u32[]{:S(2)}, u32[]{:S(2)}) async-start(bf16[2,8,96,768]{3,2,0,1:T(8,128)(2,1)} %copy.184), calls=%async_computation.1 | async-start | bytes 4718592 | tf_op jit(solution)/shard_map/all_to_all | solution.py:180
  587.7 29.7 %copy-start.36 = (s32[1024]{0:T(1024)}, s32[1024]{0:T(1024)S(1)}, u32[]{:S(2)}) copy-start(s32[1024]{0:T(1024)S(1)} %broadcast_clamp_fusion) | copy-start | bytes 12292
  632.5 33.1 %all-to-all-start.2 = ((bf16[2,8,96,768]{3,2,0,1:T(8,128)(2,1)}), bf16[2,8,96,768]{3,2,0,1:T(8,128)(2,1)S(1)}, u32[]{:S(2)}, u32[]{:S(2)}) async-start(bf16[2,8,96,768]{3,2,0,1:T(8,128)(2,1)} %fusion.13), calls=%async_computation.2 | async-start | bytes 4718592 | tf_op jit(solution)/shard_map/all_to_all | solution.py:203
  665.6 26.3 %copy-start.4 = (bf16[2,8,96,768]{3,2,0,1:T(8,128)(2,1)}, bf16[2,8,96,768]{3,2,0,1:T(8,128)(2,1)S(1)}, u32[]{:S(2)}) copy-start(bf16[2,8,96,768]{3,2,0,1:T(8,128)(2,1)S(1)} %all-to-all-done.2) | copy-start | bytes 7077892
  665.6 26.3 %slice-start.12 = ((s8[9437184]{0:T(1024)(128)(4,1)}), s8[4194304]{0:T(1024)(128)(4,1)S(1)}, s32[]{:S(2)}) async-start(s8[9437184]{0:T(1024)(128)(4,1)} %bitcast.130), calls=%async_computation.21 | async-start | bytes 8388608
  667.3 24.6 %slice-start.13 = ((s8[9437184]{0:T(1024)(128)(4,1)}), s8[4194304]{0:T(1024)(128)(4,1)S(1)}, s32[]{:S(2)}) async-start(s8[9437184]{0:T(1024)(128)(4,1)} %bitcast.130), calls=%async_computation.22 | async-start | bytes 8388608
  667.3 24.6 %slice-start.14 = ((s8[9437184]{0:T(1024)(128)(4,1)}), s8[1048576]{0:T(1024)(128)(4,1)S(1)}, s32[]{:S(2)}) async-start(s8[9437184]{0:T(1024)(128)(4,1)} %bitcast.130), calls=%async_computation.23 | async-start | bytes 2097152
  706.3 34.8 %all-to-all-start.3 = ((bf16[2,8,96,768]{3,2,0,1:T(8,128)(2,1)}), bf16[2,8,96,768]{3,2,0,1:T(8,128)(2,1)}, u32[]{:S(2)}, u32[]{:S(2)}) async-start(bf16[2,8,96,768]{3,2,0,1:T(8,128)(2,1)} %copy.189), calls=%async_computation.3 | async-start | bytes 4718592 | tf_op jit(solution)/shard_map/all_to_all | solution.py:221
  710.8 318.5 %all-reduce.4.cloned.1.call-start = ((), (), s32[]{:S(2)}) async-start(), calls=%async_computation.8 | async-start | bytes 19922944
  751.9 16.9 %copy-start.2 = (f32[512,768]{1,0:T(8,128)S(1)}, f32[512,768]{1,0:T(8,128)}, u32[]{:S(2)}) copy-start(f32[512,768]{1,0:T(8,128)} %copy-done.1) | copy-start | bytes 4718596
  751.9 16.9 %copy-start.30 = (f32[768]{0:T(1024)S(1)}, f32[768]{0:T(1024)}, u32[]{:S(2)}) copy-start(f32[768]{0:T(1024)} %copy-done.29) | copy-start | bytes 9220
  780.0 18.6 %slice-start = ((s8[12582912]{0:T(1024)(128)(4,1)}), s8[4194304]{0:T(1024)(128)(4,1)S(1)}, s32[]{:S(2)}) async-start(s8[12582912]{0:T(1024)(128)(4,1)} %bitcast.106), calls=%async_computation.9 | async-start | bytes 8388608
  780.0 18.6 %slice-start.1 = ((s8[12582912]{0:T(1024)(128)(4,1)}), s8[4194304]{0:T(1024)(128)(4,1)S(1)}, s32[]{:S(2)}) async-start(s8[12582912]{0:T(1024)(128)(4,1)} %bitcast.106), calls=%async_computation.10 | async-start | bytes 8388608
  865.0 274.2 %reduce-scatter.2.cloned.1.call-start = ((), (), s32[]{:S(2)}) async-start(), calls=%async_computation.5 | async-start | bytes 10027008 | tf_op jit(solution)/shard_map/reduce_scatter | solution.py:52
  (51 other events, 232.5 us)
Sparse Core Ops, SparseCore 0:
  12.0 310.6 all-gather.6
  325.2 143.9 all-gather.4
  865.1 164.2 all-reduce.3
  1033.6 105.4 reduce-scatter.1
where the time goes:
time: 1160 us; the launch traced here: 1150 us
  waiting for transfers between devices  629 us (54%)
  local copies, waits for them, and re-layouts  228 us (20%)
  matrix products  133 us (11%)
  other arithmetic  70.9 us (6%)
  blocking collectives  58.7 us (5%)
  between operations  15.2 us (1%)
  starting transfers between devices  13.7 us (1%)
    all_gather x1, waiting for transfers between devices, rows_first(): result = lax.all_gather(both, axis, axis=0, tiled=True)  295 us
    unnamed x5, waiting for transfers between devices  136 us
    reduce_scatter x1, waiting for transfers between devices, one_scatter(): lax.psum_scatter(lines, axis, tiled=True).reshape(-1)  103 us
    all_to_all x1, blocking collectives, shards(): lax.all_to_all(slot_rows.reshape(2, groups, capacity, width), 'narrow', s...  58.7 us
    all_gather x1, waiting for transfers between devices, gather_together(): lines, at, gathered = (lax.all_gather(ravelled, axis), 0, [])  46.1 us
    unnamed x139, local copies, waits for them, and re-layouts  30.2 us
    all_to_all x1, waiting for transfers between devices, shards(): lax.all_to_all(d_slot_out.reshape(2, groups, capacity, width), 'narrow',...  27.8 us
    dot_general x1, matrix products, shards(): jnp.einsum('krd,kfd->krf', d_rows_out, down_all_b, preferred_element_type...  24.6 us
  transfers between devices with their start and end apart: 7, of which 6 were waited for; matrix products, arithmetic and copies ran while one was open for 11% of the time, Pallas kernels for 0%

commit v1 on v0

v1 whole, which is shorter than its diff:
```python
import jax
import jax.numpy as jnp
from jax import lax
from jax.sharding import Mesh
from jax.sharding import PartitionSpec as P

HEAD = 64
TOP = 2
SIZES = (4, 2, 2, 4, 2)
NAMES = ("x", "yh", "c", "z", "yl")
WIDE = ("x", "yh", "c")
NARROW = ("z", "yl")
BF = jnp.bfloat16
F32 = jnp.float32


def shift(value, axis, by):
    count = lax.axis_size(axis)
    return lax.ppermute(value, axis, [(i, (i + by) % count) for i in range(count)])


def ordered(mine, other, index):
    first = jnp.where(index == 0, mine, other)
    second = jnp.where(index == 0, other, mine)
    return first, second


def gather_dense(block):
    width = block.shape[1]
    spread = jnp.broadcast_to(block[None], (8, 8, width))
    near = lax.all_to_all(spread, NARROW, split_axis=0, concat_axis=0, tiled=True)
    rows = near[:, :6].reshape(48, width)
    x, yh, c = (lax.axis_index(name) for name in WIDE)
    both = jnp.stack(ordered(rows, shift(rows, "yh", 1), yh))
    full = jnp.zeros((4, 2, 2, 48, width), BF)
    for step in range(4):
        part = both if step == 0 else shift(both, "x", step)
        pair = jnp.stack(ordered(part, shift(part, "c", 1), c), 1)
        full = lax.dynamic_update_slice(full, pair[None], ((x - step) % 4, 0, 0, 0, 0))
    return full.reshape(768, width)


def scatter_dense(grad):
    width = grad.shape[1]
    x, yh, c = (lax.axis_index(name) for name in WIDE)
    parts = grad.reshape(8, 2, 48, width)
    keep = lax.dynamic_index_in_dim(parts, c, 1, False)
    away = lax.dynamic_index_in_dim(parts, 1 - c, 1, False)
    held = (keep.astype(F32) + shift(away, "c", 1).astype(F32)).astype(BF).reshape(4, 2, 48, width)
    total = lax.dynamic_index_in_dim(held, x, 0, False).astype(F32)
    for step in (1, 3, 2):
        piece = lax.dynamic_index_in_dim(held, (x + step) % 4, 0, False)
        total = total + shift(piece, "x", step).astype(F32)
    away = lax.dynamic_index_in_dim(total, 1 - yh, 0, False).astype(BF)
    total = lax.dynamic_index_in_dim(total, yh, 0, False) + shift(away, "yh", 1).astype(F32)
    pieces = total.astype(BF).reshape(8, 6, width)
    pieces = jnp.pad(pieces, ((0, 0), (0, 2), (0, 0)))
    near = lax.all_to_all(pieces, NARROW, split_axis=0, concat_axis=0, tiled=True)
    return jnp.sum(near.astype(F32), 0)[:6]


def layer_norm(values, gain_row, bias_row):
    average = jnp.mean(values, -1, keepdims=True)
    centered = values - average
    variance = jnp.mean(centered * centered, -1, keepdims=True)
    return centered * lax.rsqrt(variance + 1e-05) * gain_row + bias_row


def smooth_act(pre_act):
    return jax.nn.gelu(pre_act, approximate=True)


def visible(lengths_row, mask_row, count):
    places = lax.iota(jnp.int32, count)
    seq_ends = jnp.cumsum(lengths_row)
    segment = jnp.sum((places[:, None] >= seq_ends[None, :]).astype(jnp.int32), 1)
    same_seq = segment[:, None] == segment[None, :]
    causal = places[None, :] <= places[:, None]
    open_key = (mask_row[None, :] == 1) | (places[:, None] == places[None, :])
    return same_seq & causal & open_key


def masked_scores(q_part, k_part, allowed):
    scores = jnp.einsum("qhd,khd->hqk", q_part, k_part, preferred_element_type=F32) * 0.125
    return jnp.where(allowed[None], scores, -1e30)


def with_tail(rows, values):
    high = values.astype(BF)
    low = (values - high.astype(F32)).astype(BF)
    line = jnp.concatenate((jnp.pad(high, ((0, 0), (0, 32))), jnp.pad(low, ((0, 0), (0, 32)))), 1)
    tail = jnp.pad(line[:, None, :], ((0, 0), (0, 15), (0, 512)))
    return jnp.concatenate((rows, tail), 1)


def split_tail(sent):
    line = sent[:, 96].astype(F32)
    return sent[:, :96], line[:, :96] + line[:, 128:224]


def exchange(rows):
    return lax.all_to_all(rows, ("c", "z", "yl"), split_axis=0, concat_axis=0, tiled=True)


def shards(
    tokens,
    seq_lengths,
    key_mask,
    routes,
    cotangent,
    qkv_weight,
    out_weight,
    router_weight,
    norm_gains,
    norm_biases,
    up_train,
    down_train,
    up_frozen,
    down_frozen,
):
    row_count, width = tokens.shape
    head_count = width // HEAD
    experts = 16
    capacity = 96
    slot_count = experts * capacity
    core = lax.axis_index("c")

    small = jnp.concatenate((router_weight, norm_gains.T, norm_biases.T), 1).astype(BF)
    block = jnp.concatenate(
        (qkv_weight.astype(BF), out_weight.astype(BF), jnp.pad(small, ((0, 0), (0, 108)))), 1
    )
    dense = gather_dense(jnp.pad(block, ((0, 2), (0, 0))))
    w_qkv, w_out, rest = dense[:, :2304], dense[:, 2304:3072], dense[:, 3072:]
    w_router = rest[:, :16]
    gains = rest[:, 16:18].astype(F32).T
    biases = rest[:, 18:20].astype(F32).T

    up_t, down_t = up_train[0].astype(BF), down_train[0].astype(BF)
    up_f, down_f = up_frozen[0], down_frozen[0]
    up_other = shift(jnp.where(core == 0, up_f, up_t), "c", 1)
    down_other = shift(jnp.where(core == 0, down_f, down_t), "c", 1)
    up_two = jnp.concatenate(ordered(jnp.where(core == 0, up_t, up_f), up_other, core), 0)
    down_two = jnp.concatenate(ordered(jnp.where(core == 0, down_t, down_f), down_other, core), 0)
    w_up = lax.all_gather(up_two, ("x", "yh"), tiled=True)
    w_down = lax.all_gather(down_two, ("x", "yh"), tiled=True)

    route_hot = routes[:, :, None] == lax.iota(jnp.int32, experts)[None, None, :]
    token_hot = jnp.any(route_hot, 1).astype(BF)
    places = lax.iota(jnp.int32, row_count)
    before = (places[None, :] < places[:, None]).astype(BF)
    earlier = jnp.dot(before, token_hot, preferred_element_type=F32)
    slot_pos = jnp.sum(jnp.where(route_hot, earlier[:, None, :], 0.0), -1).astype(jnp.int32)
    slot_id = jnp.where(slot_pos < capacity, routes * capacity + slot_pos, slot_count)
    slots = lax.iota(jnp.int32, slot_count)
    hot_first = slots[:, None] == slot_id[None, :, 0]
    hot_second = slots[:, None] == slot_id[None, :, 1]
    dispatch = (hot_first | hot_second).astype(BF)
    g_slots = jnp.dot(dispatch, cotangent, preferred_element_type=F32).astype(BF)
    g_rows = exchange(g_slots.reshape(experts, capacity, width)).reshape(slot_count, width)

    allowed = visible(seq_lengths[0], key_mask, row_count)
    x_in = tokens.astype(F32)
    h_one = layer_norm(x_in, gains[0], biases[0]).astype(BF)
    qkv_all = jnp.dot(h_one, w_qkv, preferred_element_type=F32).astype(BF)
    q_part = qkv_all[:, :width].reshape(row_count, head_count, HEAD)
    k_part = qkv_all[:, width : 2 * width].reshape(row_count, head_count, HEAD)
    v_part = qkv_all[:, 2 * width :].reshape(row_count, head_count, HEAD)
    scores = masked_scores(q_part, k_part, allowed)
    row_peak = jnp.max(scores, -1, keepdims=True)
    exp_scores = jnp.exp(scores - row_peak)
    row_total = jnp.sum(exp_scores, -1, keepdims=True)
    log_total = row_peak + jnp.log(row_total)
    attn_probs = (exp_scores / row_total).astype(BF)
    attn_out = (
        jnp.einsum("hqk,khd->qhd", attn_probs, v_part, preferred_element_type=F32)
        .reshape(row_count, width)
        .astype(BF)
    )
    x_mid = x_in + jnp.dot(attn_out, w_out, preferred_element_type=F32)
    h_two = layer_norm(x_mid, gains[1], biases[1]).astype(BF)
    logits = jnp.dot(h_two, w_router, preferred_element_type=F32)
    chosen = jnp.sum(jnp.where(route_hot, logits[:, None, :], 0.0), -1)
    gate_vals = jax.nn.softmax(chosen, -1)
    gate_slot = jnp.sum(
        jnp.where(hot_first, gate_vals[None, :, 0], 0.0)
        + jnp.where(hot_second, gate_vals[None, :, 1], 0.0),
        1,
    )
    h_slots = jnp.dot(dispatch, h_two, preferred_element_type=F32).astype(BF)
    sent = with_tail(h_slots.reshape(experts, capacity, width), gate_slot.reshape(experts, capacity))
    rows, gate_rows = split_tail(exchange(sent))
    rows = rows.reshape(slot_count, width)
    gate_rows = gate_rows.reshape(slot_count, 1)

    up_vals = jnp.dot(rows, w_up, preferred_element_type=F32)
    act_vals, gelu_pull = jax.vjp(smooth_act, up_vals)
    activated = act_vals.astype(BF)
    expert_out = jnp.dot(activated, w_down, preferred_element_type=F32).astype(BF)
    d_out = (gate_rows * g_rows.astype(F32)).astype(BF)
    d_gate_rows = jnp.sum(expert_out.astype(F32) * g_rows.astype(F32), -1)
    d_acts = jnp.einsum("rd,fd->rf", d_out, w_down, preferred_element_type=F32)
    d_up = gelu_pull(d_acts)[0].astype(BF)
    d_rows = jnp.einsum("rf,df->rd", d_up, w_up, preferred_element_type=F32).astype(BF)
    d_sent = with_tail(
        d_rows.reshape(experts, capacity, width), d_gate_rows.reshape(experts, capacity)
    )
    d_back, d_gate_slot = split_tail(exchange(d_sent))
    returned = exchange(expert_out.reshape(experts, capacity, width)).reshape(slot_count, width)
    grad_down_t = jnp.einsum("rf,rd->fd", activated, d_out, preferred_element_type=F32).astype(BF)
    grad_up_t = jnp.einsum("rd,rf->df", rows, d_up, preferred_element_type=F32).astype(BF)

    def expert_grad(grad):
        parts = grad.reshape(8, 2, grad.shape[0] // 16, grad.shape[1])
        got = lax.ppermute(parts[:, 1], "c", [(0, 1)])
        mine = jnp.where(core == 0, parts[:, 0], got).reshape(-1, grad.shape[1])
        return lax.psum_scatter(mine, ("x", "yh"), scatter_dimension=0, tiled=True).astype(F32)[None]

    grad_up = expert_grad(grad_up_t)
    grad_down = expert_grad(grad_down_t)

    pick = (slot_id[:, :, None] == slots[None, None, :]).astype(BF)
    back_first = jnp.dot(pick[:, 0], returned, preferred_element_type=F32)
    back_second = jnp.dot(pick[:, 1], returned, preferred_element_type=F32)
    block_out = (x_mid + gate_vals[:, :1] * back_first + gate_vals[:, 1:] * back_second).astype(BF)
    d_res = cotangent.astype(F32)
    d_gate_flat = d_gate_slot.reshape(slot_count)
    d_gates = jnp.sum(
        jnp.where(slot_id[:, :, None] == slots[None, None, :], d_gate_flat[None, None, :], 0.0), -1
    )
    d_chosen = gate_vals * (d_gates - jnp.sum(gate_vals * d_gates, -1, keepdims=True))
    d_logits = jnp.sum(jnp.where(route_hot, d_chosen[:, :, None], 0.0), 1)
    d_h_two = jnp.dot(
        pick[:, 0] + pick[:, 1], d_back.reshape(slot_count, width), preferred_element_type=F32
    )
    d_h_two = d_h_two + jnp.einsum("re,de->rd", d_logits, w_router.astype(F32))
    grad_router_l = jnp.einsum("rd,re->de", h_two.astype(F32), d_logits)
    unused_two, pull_two = jax.vjp(layer_norm, x_mid, gains[1], biases[1])
    d_mid_norm, d_gain_two, d_bias_two = pull_two(d_h_two)
    d_x_mid = d_res + d_mid_norm
    d_proj = d_x_mid.astype(BF)
    grad_out_l = jnp.einsum("rd,re->de", attn_out, d_proj, preferred_element_type=F32)
    d_attn = jnp.einsum("re,de->rd", d_proj, w_out, preferred_element_type=F32).astype(BF)
    d_attn_h = d_attn.reshape(row_count, head_count, HEAD)
    probs_back = jnp.exp(masked_scores(q_part, k_part, allowed) - log_total)
    d_probs = jnp.einsum("qhd,khd->hqk", d_attn_h, v_part, preferred_element_type=F32)
    d_vals = jnp.einsum(
        "hqk,qhd->khd", probs_back.astype(BF), d_attn_h, preferred_element_type=F32
    )
    row_delta = jnp.sum(probs_back * d_probs, -1, keepdims=True)
    d_scores = (probs_back * (d_probs - row_delta)).astype(BF)
    d_query = jnp.einsum("hqk,khd->qhd", d_scores, k_part, preferred_element_type=F32) * 0.125
    d_key = jnp.einsum("hqk,qhd->khd", d_scores, q_part, preferred_element_type=F32) * 0.125
    d_qkv = jnp.concatenate(
        (
            d_query.reshape(row_count, width),
            d_key.reshape(row_count, width),
            d_vals.reshape(row_count, width),
        ),
        1,
    ).astype(BF)
    grad_qkv_l = jnp.einsum("rd,re->de", h_one, d_qkv, preferred_element_type=F32)
    d_h_one = jnp.einsum("re,de->rd", d_qkv, w_qkv, preferred_element_type=F32)
    unused_one, pull_one = jax.vjp(layer_norm, x_in, gains[0], biases[0])
    d_in_norm, d_gain_one, d_bias_one = pull_one(d_h_one)
    input_grad = d_x_mid + d_in_norm
    small_l = jnp.concatenate(
        (grad_router_l, jnp.stack((d_gain_one, d_gain_two, d_bias_one, d_bias_two), 1)), 1
    )
    grads = jnp.concatenate(
        (grad_qkv_l.astype(BF), grad_out_l.astype(BF), jnp.pad(small_l.astype(BF), ((0, 0), (0, 108)))), 1
    )
    own = scatter_dense(grads)
    return (
        block_out,
        input_grad,
        own[:, :2304],
        own[:, 2304:3072],
        own[:, 3072:3088],
        own[:, 3088:3090].T,
        own[:, 3090:3092].T,
        grad_up,
        grad_down,
    )


def solution(mesh):
    fine = Mesh(mesh.devices.reshape(SIZES), NAMES)
    by_row = P(NAMES, None)
    by_column = P(None, NAMES)
    by_expert = P(NARROW, WIDE, None)
    return jax.shard_map(
        shards,
        mesh=fine,
        in_specs=(by_row, by_row, P(NAMES)) + (by_row,) * 5 + (by_column,) * 2 + (by_expert,) * 4,
        out_specs=(by_row,) * 5 + (by_column,) * 2 + (by_expert,) * 2,
        check_vma=False,
    )
```

time: 1160 us -> 529 us (0.46)
  waiting for transfers between devices: 629 us -> 216 us
  local copies, waits for them, and re-layouts: 228 us -> 36.2 us
  blocking collectives: 58.7 us -> 0 us
  starting transfers between devices: 13.7 us -> 52.7 us
  other arithmetic: 70.9 us -> 56 us
  matrix products: 133 us -> 147 us
    all_gather x2, waiting for transfers between devices: 341 us -> 0.01 us  [the longest x1 0.01 us: shards(): w_up = lax.all_gather(up_two, ('x', 'yh'), tiled=True)]
    unnamed x5 -> x4, waiting for transfers between devices: 136 us -> 0.07 us
    all_to_all x3 -> x6, waiting for transfers between devices: 49 us -> 134 us  [the longest x4 119 us: exchange(): lax.all_to_all(rows, ('c', 'z', 'yl'), split_axis=0, concat_axis=0, tiled...]
    reduce_scatter x1 -> x2, waiting for transfers between devices: 103 us -> 23.3 us  [expert_grad(): lax.psum_scatter(mine, ('x', 'yh'), scatter_dimension=0, tiled=True)]
    ppermute x0 -> x17, waiting for transfers between devices: none -> 58.8 us  [the longest x15 58.8 us: shift(): lax.ppermute(value, axis, [(i, (i + by) % count) for i in range(count)])]
    all_to_all x1 -> x0, blocking collectives: 58.7 us -> none  [shards(): lax.all_to_all(slot_rows.reshape(2, groups, capacity, width), 'narrow', s...]
    another operation x19 -> x4, local copies, waits for them, and re-layouts: 43.9 us -> 0.02 us  [shards(): jnp.stack((d_gain_one, d_gain_two, d_bias_one, d_bias_two), 1)]
    reshape x15 -> x4, local copies, waits for them, and re-layouts: 32.7 us -> 1.33 us  [the longest x1 1.07 us: scatter_dense(): pieces = total.astype(BF).reshape(8, 6, width)]
  transfers between devices with their start and end apart: 7 -> 27, of which waited for: 6 -> 14; matrix products, arithmetic and copies ran while one was open for 11% -> 36% of each run, Pallas kernels for 0% -> 0%
where the time goes in v1:
time: 529 us; the launch traced here: 523 us
  waiting for transfers between devices  216 us (41%)
  matrix products  147 us (28%)
  other arithmetic  56 us (11%)
  starting transfers between devices  52.7 us (10%)
  local copies, waits for them, and re-layouts  36.2 us (7%)
  between operations  15.4 us (3%)
    all_to_all x4, waiting for transfers between devices, exchange(): lax.all_to_all(rows, ('c', 'z', 'yl'), split_axis=0, concat_axis=0, tiled...  119 us
    ppermute x15, waiting for transfers between devices, shift(): lax.ppermute(value, axis, [(i, (i + by) % count) for i in range(count)])  58.8 us
    reduce_scatter x2, waiting for transfers between devices, expert_grad(): lax.psum_scatter(mine, ('x', 'yh'), scatter_dimension=0, tiled=True)  23.3 us
    dot_general x1, matrix products, shards(): d_acts = jnp.einsum('rd,fd->rf', d_out, w_down, preferred_element_type=F32)  22.3 us
    all_to_all x4, starting transfers between devices, exchange(): lax.all_to_all(rows, ('c', 'z', 'yl'), split_axis=0, concat_axis=0, tiled...  18.8 us
    dot_general x1, matrix products, shards(): jnp.dot(activated, w_down, preferred_element_type=F32).astype(BF)  17.9 us
    ppermute x15, starting transfers between devices, shift(): lax.ppermute(value, axis, [(i, (i + by) % count) for i in range(count)])  16.1 us
    dot_general x1, matrix products, shards(): jnp.einsum('rf,rd->fd', activated, d_out, preferred_element_type=F32)  14.9 us
  transfers between devices with their start and end apart: 27, of which 14 were waited for; matrix products, arithmetic and copies ran while one was open for 36% of the time, Pallas kernels for 0%

profile of v1, /device:TPU:0, one launch (start us, length us, event | category | flops | bytes accessed | tf_op | source)
XLA Modules:
  0.0 523.2 jit_solution(4178921321959896142)
XLA Ops:
  13.4 6.4 %all-to-all-start = ((bf16[8,8,3200]{2,1,0:T(8,128)(2,1)}), bf16[8,8,3200]{2,1,0:T(8,128)(2,1)S(1)}, u32[]{:S(2)}, u32[]{:S(2)}) async-start(bf16[8,8,3200]{2,1,0:T(8,128)(2,1)} %broadcast_in_dim.172), calls=%async_computation | async-start | bytes 819200 | tf_op jit(solution)/shard_map/all_to_all | solution.py:31
  21.7 7.3 %all-to-all-done = bf16[8,8,3200]{2,1,0:T(8,128)(2,1)S(1)} async-done(((bf16[8,8,3200]{2,1,0:T(8,128)(2,1)}), bf16[8,8,3200]{2,1,0:T(8,128)(2,1)S(1)}, u32[]{:S(2)}, u32[]{:S(2)}) %all-to-all-start) | async-done | bytes 409632 | tf_op jit(solution)/shard_map/all_to_all | solution.py:31
  32.5 9.8 %collective-permute-done = bf16[48,3200]{1,0:T(8,128)(2,1)S(1)} collective-permute-done((bf16[48,3200]{1,0:T(8,128)(2,1)S(1)}, bf16[48,3200]{1,0:T(8,128)(2,1)S(1)}, u32[]{:S(2)}, u32[]{:S(2)}) %collective-permute-start) | collective-permute-done | bytes 307232 | tf_op jit(solution)/shard_map/ppermute | solution.py:19
  50.9 14.7 %collective-permute-done.2 = bf16[2,48,3200]{2,1,0:T(8,128)(2,1)} collective-permute-done((bf16[2,48,3200]{2,1,0:T(8,128)(2,1)}, bf16[2,48,3200]{2,1,0:T(8,128)(2,1)}, u32[]{:S(2)}, u32[]{:S(2)}) %collective-permute-start.2) | collective-permute-done | bytes 614432 | tf_op jit(solution)/shard_map/ppermute | solution.py:19
  66.9 19.3 %collective-permute-done.4 = bf16[2,48,3200]{2,1,0:T(8,128)(2,1)S(1)} collective-permute-done((bf16[2,48,3200]{2,1,0:T(8,128)(2,1)}, bf16[2,48,3200]{2,1,0:T(8,128)(2,1)S(1)}, u32[]{:S(2)}, u32[]{:S(2)}) %collective-permute-start.4) | collective-permute-done | bytes 614432 | tf_op jit(solution)/shard_map/ppermute | solution.py:19
  86.1 5.2 collective-permute-done.6
  120.6 4.8 all-to-all-start.1
  128.4 52.6 %all-to-all-done.1 = bf16[16,112,768]{2,1,0:T(8,128)(2,1)} async-done(((bf16[16,112,768]{2,1,0:T(8,128)(2,1)}), bf16[16,112,768]{2,1,0:T(8,128)(2,1)}, u32[]{:S(2)}, u32[]{:S(2)}) %all-to-all-start.1) | async-done | bytes 2752544 | tf_op jit(solution)/shard_map/all_to_all | solution.py:102
  181.1 5.1 all-to-all-start.3
  190.5 13.8 %fusion.110 = f32[1536,3072]{1,0:T(8,128)} fusion(bf16[1536,768]{1,0:T(8,128)(2,1)} %bitcast.226, bf16[768,3072]{1,0:T(8,128)(2,1)} %all-gather.3.cloned.1.call-done), kind=kOutput, calls=%fused_computation.238 | convolution fusion | flops 7247757312 | bytes 25952256 | tf_op jit(solution)/shard_map/dot_general | solution.py:195
  204.3 12.6 %all-to-all-done.3 = bf16[16,96,768]{2,1,0:T(8,128)(2,1)} async-done(((bf16[16,96,768]{2,1,0:T(8,128)(2,1)}), bf16[16,96,768]{2,1,0:T(8,128)(2,1)}, u32[]{:S(2)}, u32[]{:S(2)}) %all-to-all-start.3) | async-done | bytes 2359328 | tf_op jit(solution)/shard_map/all_to_all | solution.py:102
  216.9 17.9 %fusion.18 = (bf16[1536,768]{1,0:T(8,128)(2,1)S(1)}, f32[1536]{0:T(1024)S(1)}, bf16[1536,768]{1,0:T(8,128)(2,1)}) fusion(bf16[16,96,768]{2,1,0:T(8,128)(2,1)} %all-to-all-done.3, f32[1536]{0:T(1024)S(1)} %mul.253, bf16[3072,768]{1,0:T(8,128)(2,1)} %all-gather.5.cloned.1.call-done, f32[1536,3072]{1,0:T(8,128)} %fusion.110), kind=kOutput, calls=%fused_computation.36 | convolution fusion | flops 7298480640 | bytes 30683136 | tf_op jit(solution)/shard_map/dot_general | solution.py:198
  234.8 14.9 %convolution_convert_fusion = bf16[3072,768]{1,0:T(8,128)(2,1)S(1)} fusion(bf16[1536,768]{1,0:T(8,128)(2,1)S(1)} %get-tuple-element.78, f32[1536,3072]{1,0:T(8,128)} %fusion.110), kind=kOutput, calls=%fused_computation.30 | convolution fusion | flops 7292583936 | bytes 25952256 | tf_op jit(solution)/shard_map/rf,rd->fd/dot_general | solution.py:209
  256.5 22.3 %fusion.6 = bf16[1536,3072]{1,0:T(8,128)(2,1)S(1)} fusion(f32[1536,3072]{1,0:T(8,128)} %fusion.110, bf16[1536,768]{1,0:T(8,128)(2,1)} %copy-done.57, bf16[3072,768]{1,0:T(8,128)(2,1)} %all-gather.5.cloned.1.call-done), kind=kOutput, calls=%fused_computation.8 | convolution fusion | flops 7342129152 | bytes 35389440 | tf_op jit(solution)/shard_map/rd,fd->rf/dot_general | solution.py:201
  278.9 7.9 %convolution_convert_fusion.4 = bf16[1536,768]{1,0:T(8,128)(2,1)S(1)} fusion(bf16[1536,3072]{1,0:T(8,128)(2,1)S(1)} %fusion.6, bf16[768,3072]{1,0:T(8,128)(2,1)S(1)} %bitcast.247), kind=kOutput, calls=%fused_computation.40 | convolution fusion | flops 7248936960 | bytes 16515072 | tf_op jit(solution)/shard_map/rf,df->rd/dot_general | solution.py:203
  299.4 33.5 %all-to-all-done.4 = bf16[16,112,768]{2,1,0:T(8,128)(2,1)} async-done(((bf16[16,112,768]{2,1,0:T(8,128)(2,1)}), bf16[16,112,768]{2,1,0:T(8,128)(2,1)}, u32[]{:S(2)}, u32[]{:S(2)}) %all-to-all-start.4) | async-done | bytes 2752544 | tf_op jit(solution)/shard_map/all_to_all | solution.py:102
  347.7 13.7 %multiply_reduce_fusion = (f32[12,512]{1,0:T(8,128)S(1)}, f32[12,512,512]{1,2,0:T(8,128)}) fusion(f32[12,512]{1,0:T(8,128)S(1)} %log_add_fusion, f32[12,512,512]{1,2,0:T(8,128)} %copy-done, pred[512,512]{0,1:T(8,128)(4,1)S(1)} %fusion.60, bf16[512,12,64]{0,2,1:T(8,128)(2,1)} %bitcast.219, bf16[512,12,64]{0,2,1:T(8,128)(2,1)} %bitcast.218), kind=kOutput, calls=%fused_computation.11 | convolution fusion | flops 418375680 | bytes 27049984 | tf_op jit(solution)/shard_map/qhd,khd->hqk/dot_general | solution.py:245
  361.4 7.6 %multiply_convert_fusion.1 = bf16[12,512,512]{1,2,0:T(8,128)(2,1)S(1)} fusion(f32[12,512,512]{1,2,0:T(8,128)} %get-tuple-element.112, f32[12,512]{1,0:T(8,128)S(1)} %get-tuple-element.111, f32[12,512]{1,0:T(8,128)S(1)} %log_add_fusion, f32[12,512,512]{1,2,0:T(8,128)S(1)} %bitcast.193, pred[512,512]{0,1:T(8,128)(4,1)S(1)} %fusion.60), kind=kLoop, calls=%fused_computation.10 | loop fusion | flops 18874368 | bytes 31768576 | tf_op jit(solution)/shard_map/convert_element_type | solution.py:250
  393.6 10.4 %convolution_convert_fusion.2 = bf16[768,3072]{1,0:T(8,128)(2,1)S(1)} fusion(bf16[1536,768]{1,0:T(8,128)(2,1)S(1)} %bitcast.227, bf16[1536,3072]{1,0:T(8,128)(2,1)} %copy-done.56), kind=kOutput, calls=%fused_computation.32 | convolution fusion | flops 7250116608 | bytes 16515072 | tf_op jit(solution)/shard_map/rd,rf->df/dot_general | solution.py:210
  428.4 20.5 %all-to-all-done.2 = bf16[16,96,768]{2,1,0:T(8,128)(2,1)} async-done(((bf16[16,96,768]{2,1,0:T(8,128)(2,1)}), bf16[16,96,768]{2,1,0:T(8,128)(2,1)}, u32[]{:S(2)}, u32[]{:S(2)}) %all-to-all-start.2) | async-done | bytes 2359328 | tf_op jit(solution)/shard_map/all_to_all | solution.py:102
  463.9 4.9 collective-permute-done.14
  471.4 4.5 all-to-all-start.5
  479.2 7.1 %all-to-all-done.5 = bf16[8,8,3200]{2,1,0:T(8,128)(2,1)S(1)} async-done(((bf16[8,8,3200]{2,1,0:T(8,128)(2,1)}), bf16[8,8,3200]{2,1,0:T(8,128)(2,1)S(1)}, u32[]{:S(2)}, u32[]{:S(2)}) %all-to-all-start.5) | async-done | bytes 409632 | tf_op jit(solution)/shard_map/all_to_all | solution.py:58
  491.4 23.3 %reduce-scatter.3.cloned.1.call-done = bf16[48,3072]{1,0:T(8,128)(2,1)} async-done(((bf16[384,3072]{1,0:T(8,128)(2,1)}), bf16[48,3072]{1,0:T(8,128)(2,1)}) %reduce-scatter.3.cloned.1.call-update) | async-done | bytes 294928 | tf_op jit(solution)/shard_map/reduce_scatter | solution.py:216
  (314 shorter events, 167.6 us)
Async XLA Ops:
  7.2 183.3 %all-gather.3.cloned.1.call-start = ((), (), s32[]{:S(2)}) async-start(), calls=%async_computation.8 | async-start | bytes 5308416 | tf_op jit(solution)/shard_map/all_gather | solution.py:144
  13.4 15.7 %all-to-all-start = ((bf16[8,8,3200]{2,1,0:T(8,128)(2,1)}), bf16[8,8,3200]{2,1,0:T(8,128)(2,1)S(1)}, u32[]{:S(2)}, u32[]{:S(2)}) async-start(bf16[8,8,3200]{2,1,0:T(8,128)(2,1)} %broadcast_in_dim.172), calls=%async_computation | async-start | bytes 819200 | tf_op jit(solution)/shard_map/all_to_all | solution.py:31
  19.8 197.0 %all-gather.5.cloned.1.call-start = ((), (), s32[]{:S(2)}) async-start(), calls=%async_computation.9 | async-start | bytes 5308416 | tf_op jit(solution)/shard_map/all_gather | solution.py:145
  20.6 24.1 %collective-permute-start.9 = (bf16[192,768]{1,0:T(8,128)(2,1)}, bf16[192,768]{1,0:T(8,128)(2,1)}, u32[]{:S(2)}, u32[]{:S(2)}) collective-permute-start(bf16[192,768]{1,0:T(8,128)(2,1)} %select_bitcast_fusion.10), channel_id=1, source_target_pairs={{0,8},{8,0},{1,9},{9,1},{2,10},{10,2},{3,11},{11,3},{4,12},{12,4},... | collective-permute-start | bytes 884744 | tf_op jit(solution)/shard_map/ppermute | solution.py:19
  29.2 13.2 %collective-permute-start = (bf16[48,3200]{1,0:T(8,128)(2,1)S(1)}, bf16[48,3200]{1,0:T(8,128)(2,1)S(1)}, u32[]{:S(2)}, u32[]{:S(2)}) collective-permute-start(bf16[48,3200]{1,0:T(8,128)(2,1)S(1)} %reshape.354), channel_id=1, source_target_pairs={{0,16},{16,0},{1,17},{17,1},{2,18},{18,2},{3,19},{19,3},{4,20},{20... | collective-permute-start | bytes 921608 | tf_op jit(solution)/shard_map/ppermute | solution.py:19
  43.3 22.3 %collective-permute-start.1 = (bf16[2,48,3200]{2,1,0:T(8,128)(2,1)}, bf16[2,48,3200]{2,1,0:T(8,128)(2,1)}, u32[]{:S(2)}, u32[]{:S(2)}) collective-permute-start(bf16[2,48,3200]{2,1,0:T(8,128)(2,1)} %pad_maximum_fusion.3), channel_id=1, source_target_pairs={{0,8},{8,0},{1,9},{9,1},{2,10},{10,2},{3,11},{11,3},{4,12},{12,4},... | collective-permute-start | bytes 1843208 | tf_op jit(solution)/shard_map/ppermute | solution.py:19
  43.3 22.3 %collective-permute-start.2 = (bf16[2,48,3200]{2,1,0:T(8,128)(2,1)}, bf16[2,48,3200]{2,1,0:T(8,128)(2,1)}, u32[]{:S(2)}, u32[]{:S(2)}) collective-permute-start(bf16[2,48,3200]{2,1,0:T(8,128)(2,1)} %pad_maximum_fusion.3), channel_id=1, source_target_pairs={{0,32},{32,64},{64,96},{96,0},{1,33},{33,65},{65,97},{97,1},{2,34}... | collective-permute-start | bytes 1843208 | tf_op jit(solution)/shard_map/ppermute | solution.py:19
  46.7 39.4 %collective-permute-start.4 = (bf16[2,48,3200]{2,1,0:T(8,128)(2,1)}, bf16[2,48,3200]{2,1,0:T(8,128)(2,1)S(1)}, u32[]{:S(2)}, u32[]{:S(2)}) collective-permute-start(bf16[2,48,3200]{2,1,0:T(8,128)(2,1)} %pad_maximum_fusion.3), channel_id=1, source_target_pairs={{0,64},{32,96},{64,0},{96,32},{1,65},{33,97},{65,1},{97,33},{2,66}... | collective-permute-start | bytes 1843208 | tf_op jit(solution)/shard_map/ppermute | solution.py:19
  49.5 41.9 %collective-permute-start.6 = (bf16[2,48,3200]{2,1,0:T(8,128)(2,1)}, bf16[2,48,3200]{2,1,0:T(8,128)(2,1)S(1)}, u32[]{:S(2)}, u32[]{:S(2)}) collective-permute-start(bf16[2,48,3200]{2,1,0:T(8,128)(2,1)} %pad_maximum_fusion.3), channel_id=1, source_target_pairs={{0,96},{32,0},{64,32},{96,64},{1,97},{33,1},{65,33},{97,65},{2,98}... | collective-permute-start | bytes 1843208 | tf_op jit(solution)/shard_map/ppermute | solution.py:19
  65.6 26.4 %collective-permute-start.3 = (bf16[2,48,3200]{2,1,0:T(8,128)(2,1)}, bf16[2,48,3200]{2,1,0:T(8,128)(2,1)S(1)}, u32[]{:S(2)}, u32[]{:S(2)}) collective-permute-start(bf16[2,48,3200]{2,1,0:T(8,128)(2,1)} %collective-permute-done.2), channel_id=1, source_target_pairs={{0,8},{8,0},{1,9},{9,1},{2,10},{10,2},{3,11},{11,3},{4,12},{12,4},... | collective-permute-start | bytes 1843208 | tf_op jit(solution)/shard_map/ppermute | solution.py:19
  120.6 60.5 %all-to-all-start.1 = ((bf16[16,112,768]{2,1,0:T(8,128)(2,1)}), bf16[16,112,768]{2,1,0:T(8,128)(2,1)}, u32[]{:S(2)}, u32[]{:S(2)}) async-start(bf16[16,112,768]{2,1,0:T(8,128)(2,1)} %fusion.28), calls=%async_computation.1 | async-start | bytes 5505024 | tf_op jit(solution)/shard_map/all_to_all | solution.py:102
  181.1 35.8 %all-to-all-start.3 = ((bf16[16,96,768]{2,1,0:T(8,128)(2,1)}), bf16[16,96,768]{2,1,0:T(8,128)(2,1)}, u32[]{:S(2)}, u32[]{:S(2)}) async-start(bf16[16,96,768]{2,1,0:T(8,128)(2,1)} %bitcast.228), calls=%async_computation.3 | async-start | bytes 4718592 | tf_op jit(solution)/shard_map/all_to_all | solution.py:102
  253.4 42.7 %collective-permute-start.16 = (bf16[8,192,768]{2,1,0:T(8,128)(2,1)}, bf16[8,192,768]{2,1,0:T(8,128)(2,1)}, u32[]{:S(2)}, u32[]{:S(2)}) collective-permute-start(bf16[8,192,768]{2,1,0:T(8,128)(2,1)} %slice_bitcast_fusion.4), channel_id=1, source_target_pairs={{0,8},{1,9},{2,10},{3,11},{4,12},{5,13},{6,14},{7,15},{16,24},{17,... | collective-permute-start | bytes 7077896 | tf_op jit(solution)/shard_map/ppermute | solution.py:214
  288.5 44.4 %all-to-all-start.4 = ((bf16[16,112,768]{2,1,0:T(8,128)(2,1)}), bf16[16,112,768]{2,1,0:T(8,128)(2,1)}, u32[]{:S(2)}, u32[]{:S(2)}) async-start(bf16[16,112,768]{2,1,0:T(8,128)(2,1)} %fusion.29), calls=%async_computation.4 | async-start | bytes 5505024 | tf_op jit(solution)/shard_map/all_to_all | solution.py:102
  293.0 196.6 %reduce-scatter.5.cloned.1.call-start = ((), (), s32[]{:S(2)}) async-start(), calls=%async_computation.11 | async-start | bytes 2654208 | tf_op jit(solution)/shard_map/reduce_scatter | solution.py:216
  393.6 22.5 %collective-permute-start.10 = (bf16[8,48,3200]{2,1,0:T(8,128)(2,1)}, bf16[8,48,3200]{2,1,0:T(8,128)(2,1)}, u32[]{:S(2)}, u32[]{:S(2)}) collective-permute-start(bf16[8,48,3200]{2,1,0:T(8,128)(2,1)} %dynamic-slice_bitcast_fusion), channel_id=1, source_target_pairs={{0,8},{8,0},{1,9},{9,1},{2,10},{10,2},{3,11},{11,3},{4,12},{12,4},... | collective-permute-start | bytes 7372808 | tf_op jit(solution)/shard_map/ppermute | solution.py:19
  407.8 18.8 %collective-permute-start.15 = (bf16[8,48,3072]{2,1,0:T(8,128)(2,1)}, bf16[8,48,3072]{2,1,0:T(8,128)(2,1)}, u32[]{:S(2)}, u32[]{:S(2)}) collective-permute-start(bf16[8,48,3072]{2,1,0:T(8,128)(2,1)} %slice_bitcast_fusion.6), channel_id=1, source_target_pairs={{0,8},{1,9},{2,10},{3,11},{4,12},{5,13},{6,14},{7,15},{16,24},{17,... | collective-permute-start | bytes 7077896 | tf_op jit(solution)/shard_map/ppermute | solution.py:214
  411.7 37.2 %all-to-all-start.2 = ((bf16[16,96,768]{2,1,0:T(8,128)(2,1)}), bf16[16,96,768]{2,1,0:T(8,128)(2,1)}, u32[]{:S(2)}, u32[]{:S(2)}) async-start(bf16[16,96,768]{2,1,0:T(8,128)(2,1)} %bitcast.225), calls=%async_computation.2 | async-start | bytes 4718592 | tf_op jit(solution)/shard_map/all_to_all | solution.py:102
  416.1 98.5 %reduce-scatter.3.cloned.1.call-start = ((), (), s32[]{:S(2)}) async-start(), calls=%async_computation.10 | async-start | bytes 2654208 | tf_op jit(solution)/shard_map/reduce_scatter | solution.py:216
  420.8 31.5 %collective-permute-start.11 = (bf16[2,48,3200]{2,1,0:T(8,128)(2,1)}, bf16[2,48,3200]{2,1,0:T(8,128)(2,1)}, u32[]{:S(2)}, u32[]{:S(2)}) collective-permute-start(bf16[2,48,3200]{2,1,0:T(8,128)(2,1)} %get-tuple-element.75), channel_id=1, source_target_pairs={{0,32},{32,64},{64,96},{96,0},{1,33},{33,65},{65,97},{97,1},{2,34}... | collective-permute-start | bytes 1843208 | tf_op jit(solution)/shard_map/ppermute | solution.py:19
  421.0 31.3 %collective-permute-start.12 = (bf16[2,48,3200]{2,1,0:T(8,128)(2,1)}, bf16[2,48,3200]{2,1,0:T(8,128)(2,1)}, u32[]{:S(2)}, u32[]{:S(2)}) collective-permute-start(bf16[2,48,3200]{2,1,0:T(8,128)(2,1)} %get-tuple-element.77), channel_id=1, source_target_pairs={{0,96},{32,0},{64,32},{96,64},{1,97},{33,1},{65,33},{97,65},{2,98}... | collective-permute-start | bytes 1843208 | tf_op jit(solution)/shard_map/ppermute | solution.py:19
  424.0 31.6 %collective-permute-start.13 = (bf16[2,48,3200]{2,1,0:T(8,128)(2,1)}, bf16[2,48,3200]{2,1,0:T(8,128)(2,1)}, u32[]{:S(2)}, u32[]{:S(2)}) collective-permute-start(bf16[2,48,3200]{2,1,0:T(8,128)(2,1)} %get-tuple-element.76), channel_id=1, source_target_pairs={{0,64},{32,96},{64,0},{96,32},{1,65},{33,97},{65,1},{97,33},{2,66}... | collective-permute-start | bytes 1843208 | tf_op jit(solution)/shard_map/ppermute | solution.py:19
  457.6 11.1 %collective-permute-start.14 = (bf16[48,3200]{1,0:T(8,128)(2,1)S(1)}, bf16[48,3200]{1,0:T(8,128)(2,1)S(1)}, u32[]{:S(2)}, u32[]{:S(2)}) collective-permute-start(bf16[48,3200]{1,0:T(8,128)(2,1)S(1)} %fusion.67), channel_id=1, source_target_pairs={{0,16},{16,0},{1,17},{17,1},{2,18},{18,2},{3,19},{19,3},{4,20},{20... | collective-permute-start | bytes 921608 | tf_op jit(solution)/shard_map/ppermute | solution.py:19
  471.4 14.9 %all-to-all-start.5 = ((bf16[8,8,3200]{2,1,0:T(8,128)(2,1)}), bf16[8,8,3200]{2,1,0:T(8,128)(2,1)S(1)}, u32[]{:S(2)}, u32[]{:S(2)}) async-start(bf16[8,8,3200]{2,1,0:T(8,128)(2,1)} %pad.45), calls=%async_computation.5 | async-start | bytes 819200 | tf_op jit(solution)/shard_map/all_to_all | solution.py:58
  (68 other events, 558.7 us)
Sparse Core Ops, SparseCore 0:
  12.3 83.9 all-gather.2
  99.2 95.6 all-gather.4
  299.5 82.4 reduce-scatter.4
  428.5 86.1 reduce-scatter.2

commit v2 on v1

v2 whole, which is shorter than its diff:
```python
import jax
import jax.numpy as jnp
from jax import lax
from jax.experimental import pallas as pl
from jax.experimental.pallas import tpu as pltpu
from jax.sharding import Mesh
from jax.sharding import PartitionSpec as P

SIZES = (4, 2, 2, 4, 2)
NAMES = ("x", "yh", "c", "z", "yl")
WIDE = ("x", "yh", "c")
NARROW = ("z", "yl")
BF = jnp.bfloat16
F32 = jnp.float32
ROW = 512
D = 768
FF = 3072
CAP = 96
LINE = 112
SOURCES = 4
GELU_ONE = 0.7978845608028654
GELU_CUBE = GELU_ONE * 0.044715
MIB = 1024 * 1024


def nn(a, b):
    return jnp.dot(a, b, preferred_element_type=F32)


def nt(a, b):
    return lax.dot_general(a, b, (((1,), (1,)), ((), ())), preferred_element_type=F32)


def tn(a, b):
    return lax.dot_general(a, b, (((0,), (0,)), ((), ())), preferred_element_type=F32)


def iota(shape, dim):
    return lax.broadcasted_iota(jnp.int32, shape, dim)


def hot(mask):
    return jnp.where(mask, 1.0, 0.0).astype(BF)


def like(*dims, dtype=BF):
    return jax.ShapeDtypeStruct(dims, dtype)


def cost(flops, moved, transcendentals=0):
    return pl.CostEstimate(flops=flops, bytes_accessed=moved, transcendentals=transcendentals)


def tail_of(line):
    high = line.astype(BF).astype(F32)
    low = (line - high).astype(BF).astype(F32)
    full = jnp.concatenate([high, low, jnp.zeros((1, 512), F32)], 1)
    return jnp.where(iota((16, D), 0) == 0, jnp.broadcast_to(full, (16, D)), 0.0).astype(BF)


def line_of(tail):
    line = tail.astype(F32)[0:1]
    return line[:, :128] + line[:, 128:256]


def norm(x):
    centered = x - jnp.mean(x, -1, keepdims=True)
    scale = lax.rsqrt(jnp.mean(centered * centered, -1, keepdims=True) + 1e-5)
    return centered * scale, scale


def norm_back(d_out, x_hat, scale, gain):
    t = d_out * gain
    d_in = scale * (
        t - jnp.mean(t, -1, keepdims=True) - x_hat * jnp.mean(t * x_hat, -1, keepdims=True)
    )
    return d_in, jnp.sum(d_out * x_hat, 0, keepdims=True), jnp.sum(d_out, 0, keepdims=True)


def route_body(routes_ref, cot_ref, g_ref, sid_ref, sidt_ref):
    lane = iota((ROW, 128), 1)
    r0, r1 = routes_ref[:, 0:1], routes_ref[:, 1:2]
    either = hot((lane == r0) | (lane == r1))
    earlier = nn(hot(iota((ROW, ROW), 1) < iota((ROW, ROW), 0)), either)
    p0 = jnp.sum(jnp.where(lane == r0, earlier, 0.0), 1, keepdims=True).astype(jnp.int32)
    p1 = jnp.sum(jnp.where(lane == r1, earlier, 0.0), 1, keepdims=True).astype(jnp.int32)
    columns = (
        jnp.where(p0 < CAP, r0 * CAP + p0, -1),
        jnp.where(p1 < CAP, r1 * CAP + p1, -1),
        jnp.where(p0 < CAP, r0 * LINE + p0, -1),
        jnp.where(p1 < CAP, r1 * LINE + p1, -1),
        r0,
    )
    table = jnp.broadcast_to(r1, (ROW, 128))
    for at, column in enumerate(columns):
        table = jnp.where(lane == at, column, table)
    sid_ref[...] = table
    turned = jnp.transpose(table.astype(F32))[0:8].astype(jnp.int32)
    sidt_ref[...] = turned
    for part in range(4):
        slot = iota((4 * CAP, ROW), 0) + part * 4 * CAP
        pick = hot((slot == turned[0:1]) | (slot == turned[1:2]))
        g_ref[part * 4 * CAP : (part + 1) * 4 * CAP, :] = nn(pick, cot_ref[...]).astype(BF)


def route(routes, cotangent):
    return pl.pallas_call(
        route_body,
        out_shape=[like(16 * CAP, D), like(ROW, 128, dtype=jnp.int32), like(8, ROW, dtype=jnp.int32)],
        compiler_params=pltpu.CompilerParams(vmem_limit_bytes=32 * MIB),
        cost_estimate=cost(2 * 1536 * 512 * 768, 4 * 10**6),
    )(routes, cotangent)


def forward_body(*refs):
    lens_ref, nat_ref, mask_ref, tok_ref, sid_ref, sidt_ref = refs[:6]
    pieces = refs[6:14]
    (
        w_ref, h1p_ref, qkv_ref, probs_ref, attnp_ref, xmid_ref, h2_ref, gate_ref, vec_ref,
        router_ref, sent_ref, rest_ref, attn, bias,
    ) = refs[14:]
    for at, piece in enumerate(pieces):
        w_ref[at * 96 : (at + 1) * 96, :] = piece[:, :FF]
        rest_ref[at * 96 : (at + 1) * 96, :] = piece[:, FF:]
    turn = hot(iota((D, D), 0) == nat_ref[...])
    rest = nn(turn, rest_ref[...])
    vectors = jnp.transpose(rest)[16:24]
    router_ref[...] = rest.astype(BF)
    vec_ref[...] = vectors
    x = tok_ref[...].astype(F32)
    h1 = (norm(x)[0] * vectors[0:1] + vectors[2:3]).astype(BF)
    h1p_ref[...] = nn(h1, turn).astype(BF)
    for part in range(3):
        cols = slice(part * D, (part + 1) * D)
        qkv_ref[:, cols] = nn(h1p_ref[...], w_ref[:, cols]).astype(BF)

    end_one = lens_ref[0]
    end_two = end_one + lens_ref[1]

    def segment(place):
        return (place >= end_one).astype(jnp.int32) + (place >= end_two).astype(jnp.int32)

    query, key = iota((ROW, ROW), 0), iota((ROW, ROW), 1)
    same = segment(iota((ROW, 1), 0)) == segment(iota((1, ROW), 1))
    allowed = same & (key <= query) & ((mask_ref[...] == 1) | (key == query))
    bias[...] = jnp.where(allowed, 0.0, -1e30)
    low = iota((1, 128), 1) < 64
    half = ROW // 2
    zero = jnp.zeros((), BF)

    def pair(index, carry):
        at = pl.multiple_of(index * 128, 128)
        q = qkv_ref[:, pl.ds(at, 128)] * jnp.asarray(0.125, BF)
        k = qkv_ref[:, pl.ds(D + at, 128)]
        v = qkv_ref[:, pl.ds(2 * D + at, 128)]
        out = [None, None]
        for head in range(2):
            mine = low if head == 0 else jnp.logical_not(low)
            k_mine, v_mine = jnp.where(mine, k, zero), jnp.where(mine, v, zero)
            for block in range(2):
                count, rows = half * (block + 1), slice(block * half, (block + 1) * half)
                scores = nt(q[rows], k_mine[:count]) + bias[rows, :count]
                e = jnp.exp(scores - jnp.max(scores, 1, keepdims=True))
                probs = (e * (1.0 / jnp.sum(e, 1, keepdims=True))).astype(BF)
                probs_ref[2 * index + head, rows, :count] = probs
                if block == 0:
                    probs_ref[2 * index + head, rows, count:] = jnp.zeros((half, half), BF)
                term = nn(probs, v_mine[:count])
                out[block] = term if head == 0 else out[block] + term
        for block in range(2):
            attn[block * half : (block + 1) * half, pl.ds(at, 128)] = out[block].astype(BF)
        return carry

    lax.fori_loop(0, 6, pair, 0)
    attnp_ref[...] = nn(attn[...], turn).astype(BF)
    x_mid = x + nn(attnp_ref[...], w_ref[:, 3 * D :])
    xmid_ref[...] = x_mid
    h2 = (norm(x_mid)[0] * vectors[1:2] + vectors[3:4]).astype(BF)
    h2_ref[...] = h2
    logits = nn(h2, router_ref[...])
    lane = iota((ROW, 128), 1)
    s0, s1, r0, r1 = (sid_ref[:, at : at + 1] for at in (0, 1, 4, 5))
    c0 = jnp.sum(jnp.where(lane == r0, logits, 0.0), 1, keepdims=True)
    c1 = jnp.sum(jnp.where(lane == r1, logits, 0.0), 1, keepdims=True)
    g0, g1 = 1.0 / (1.0 + jnp.exp(c1 - c0)), 1.0 / (1.0 + jnp.exp(c0 - c1))
    gate_ref[...] = jnp.where(lane == 0, g0, jnp.where(lane == 1, g1, 0.0))
    first, second = sidt_ref[2:3], sidt_ref[3:4]
    for part in range(4):
        slot = iota((4 * LINE, ROW), 0) + part * 4 * LINE
        pick = hot((slot == first) | (slot == second))
        sent_ref[part * 4 * LINE : (part + 1) * 4 * LINE, :] = nn(pick, h2_ref[...]).astype(BF)
    for expert in range(16):
        slot = lane + expert * CAP
        line = jnp.sum(
            jnp.where(slot == s0, g0, 0.0) + jnp.where(slot == s1, g1, 0.0), 0, keepdims=True
        )
        sent_ref[expert * LINE + CAP : (expert + 1) * LINE, :] = tail_of(line)


def forward(lens, nat, mask, tokens, sid, sidt, pieces):
    vmem = pl.BlockSpec(memory_space=pltpu.VMEM)
    return pl.pallas_call(
        forward_body,
        in_specs=[pl.BlockSpec(memory_space=pltpu.SMEM)] + [vmem] * 13,
        out_shape=[
            like(D, FF),
            like(ROW, D),
            like(ROW, 3 * D),
            like(12, ROW, ROW),
            like(ROW, D),
            like(ROW, D, dtype=F32),
            like(ROW, D),
            like(ROW, 128, dtype=F32),
            like(8, D, dtype=F32),
            like(D, 128),
            like(16 * LINE, D),
        ],
        scratch_shapes=[
            pltpu.VMEM((D, 128), BF),
            pltpu.VMEM((ROW, D), BF),
            pltpu.VMEM((ROW, ROW), F32),
        ],
        compiler_params=pltpu.CompilerParams(vmem_limit_bytes=56 * MIB),
        cost_estimate=cost(2 * 512 * 768 * 6000, 20 * 10**6, 12 * 512 * 512),
    )(lens, nat, mask, tokens, sid, sidt, *pieces)


def expert_body(
    sent_ref, g_ref, up_ref, down_ref, out_ref, back_ref, x_ref, dout_ref, act_ref, dup_ref
):
    for s in range(SOURCES):
        rows = slice(s * CAP, (s + 1) * CAP)
        x_ref[rows, :] = sent_ref[s, :CAP, :]
        gate = line_of(sent_ref[s, CAP:LINE, :])
        column = jnp.transpose(jnp.broadcast_to(gate, (128, 128)))[:CAP, :1]
        dout_ref[rows, :] = (g_ref[s].astype(F32) * column).astype(BF)
    x, d_out = x_ref[...], dout_ref[...]
    for part in range(FF // 256):
        cols = slice(part * 256, (part + 1) * 256)
        up = nn(x, up_ref[:, cols])
        d_act = nt(d_out, down_ref[cols, :])
        square = up * up
        t = jnp.tanh(up * (GELU_ONE + GELU_CUBE * square))
        a = 0.5 + 0.5 * t
        act_ref[:, cols] = (up * a).astype(BF)
        slope = a + (up * (1.0 - t * t)) * (0.5 * GELU_ONE + 1.5 * GELU_CUBE * square)
        dup_ref[:, cols] = (d_act * slope).astype(BF)
    for part in range(D // 256):
        cols = slice(part * 256, (part + 1) * 256)
        out = nn(act_ref[...], down_ref[:, cols]).astype(BF)
        back = nt(dup_ref[...], up_ref[cols, :]).astype(BF)
        for s in range(SOURCES):
            out_ref[s, :, cols] = out[s * CAP : (s + 1) * CAP]
            back_ref[s, :CAP, cols] = back[s * CAP : (s + 1) * CAP]
    for s in range(SOURCES):
        d_gate = jnp.sum(out_ref[s].astype(F32) * g_ref[s].astype(F32), -1, keepdims=True)
        wide = jnp.concatenate(
            [jnp.broadcast_to(d_gate, (CAP, 128)), jnp.zeros((128 - CAP, 128), F32)], 0
        )
        back_ref[s, CAP:LINE, :] = tail_of(jnp.transpose(wide)[0:1])


def experts(sent, g, w_up, w_down):
    rows = SOURCES * CAP
    once = pl.Buffered(1)
    by_source = lambda size: pl.BlockSpec((SOURCES, size, D), lambda i: (i, 0, 0))
    by_rows = lambda width: pl.BlockSpec((rows, width), lambda i: (i, 0))
    return pl.pallas_call(
        expert_body,
        grid=(16 // SOURCES,),
        in_specs=[
            by_source(LINE),
            by_source(CAP),
            pl.BlockSpec((D, FF), lambda i: (0, 0), pipeline_mode=once),
            pl.BlockSpec((FF, D), lambda i: (0, 0), pipeline_mode=once),
        ],
        out_specs=[
            by_source(CAP), by_source(LINE), by_rows(D), by_rows(D), by_rows(FF), by_rows(FF),
        ],
        out_shape=[
            like(16, CAP, D),
            like(16, LINE, D),
            like(16 * CAP, D),
            like(16 * CAP, D),
            like(16 * CAP, FF),
            like(16 * CAP, FF),
        ],
        compiler_params=pltpu.CompilerParams(vmem_limit_bytes=60 * MIB),
        cost_estimate=cost(8 * 1536 * 768 * 3072, 40 * 10**6, 1536 * 3072),
    )(sent, g, w_up, w_down)


def back_one_body(
    nat_ref, sid_ref, dback_ref, gate_ref, router_ref, vec_ref, cot_ref, xmid_ref, h2_ref,
    attnp_ref, w_ref, dxm_ref, dattn_ref, grads_ref,
):
    lane = iota((ROW, 128), 1)
    s0, s1, w0, w1, r0, r1 = (sid_ref[:, at : at + 1] for at in range(6))
    a0 = a1 = jnp.zeros((ROW, 128), F32)
    for expert in range(16):
        line = line_of(dback_ref[expert * LINE + CAP : (expert + 1) * LINE, :])
        slot = jnp.where(lane < CAP, lane + expert * CAP, -2)
        a0 = a0 + jnp.where(slot == s0, line, 0.0)
        a1 = a1 + jnp.where(slot == s1, line, 0.0)
    dg0, dg1 = jnp.sum(a0, 1, keepdims=True), jnp.sum(a1, 1, keepdims=True)
    g0, g1 = gate_ref[:, 0:1], gate_ref[:, 1:2]
    both = g0 * dg0 + g1 * dg1
    d_logits = jnp.where(lane == r0, g0 * (dg0 - both), 0.0)
    d_logits = d_logits + jnp.where(lane == r1, g1 * (dg1 - both), 0.0)
    high = d_logits.astype(BF)
    low = (d_logits - high.astype(F32)).astype(BF)
    d_h2 = nt(high, router_ref[...]) + nt(low, router_ref[...])
    for part in range(4):
        slot = iota((ROW, 4 * LINE), 1) + part * 4 * LINE
        pick = hot((slot == w0) | (slot == w1))
        d_h2 = d_h2 + nn(pick, dback_ref[part * 4 * LINE : (part + 1) * 4 * LINE, :])
    x_hat, scale = norm(xmid_ref[...])
    d_in, d_gain, d_bias = norm_back(d_h2, x_hat, scale, vec_ref[1:2])
    d_x_mid = cot_ref[...].astype(F32) + d_in
    dxm_ref[...] = d_x_mid
    d_proj = d_x_mid.astype(BF)
    turn = hot(iota((D, D), 0) == nat_ref[...])
    dattn_ref[...] = nt(nt(d_proj, w_ref[...]).astype(BF), turn).astype(BF)
    grads_ref[:, :D] = tn(attnp_ref[...], d_proj).astype(BF)
    d_router = tn(h2_ref[...], high) + tn(h2_ref[...], low)
    sub = iota((128, D), 0)
    rows = jnp.where(sub == 17, d_gain, 0.0) + jnp.where(sub == 19, d_bias, 0.0)
    small = d_router + jnp.transpose(rows)
    grads_ref[:, D:] = tn(turn, small.astype(BF)).astype(BF)


def back_one(nat, sid, d_back, gate, router, vec, cotangent, x_mid, h2, attnp, w):
    vmem = pl.BlockSpec(memory_space=pltpu.VMEM)
    return pl.pallas_call(
        back_one_body,
        grid=(1,),
        in_specs=[vmem] * 10 + [pl.BlockSpec((D, D), lambda i: (0, 3))],
        out_specs=[vmem] * 3,
        out_shape=[like(ROW, D, dtype=F32), like(ROW, D), like(D, D + 128)],
        compiler_params=pltpu.CompilerParams(vmem_limit_bytes=48 * MIB),
        cost_estimate=cost(2 * 512 * 768 * 4300, 12 * 10**6),
    )(nat, sid, d_back, gate, router, vec, cotangent, x_mid, h2, attnp, w)


def back_two_body(
    nat_ref, dattn_ref, probs_ref, qkv_ref, h1p_ref, dxm_ref, tok_ref, vec_ref, w_ref,
    gx_ref, grads_ref, d_qkv,
):
    low = iota((1, 128), 1) < 64
    zero = jnp.zeros((), BF)
    half = ROW // 2

    def add(terms, at, term):
        terms[at] = term if terms[at] is None else terms[at] + term

    def pair(index, carry):
        at = pl.multiple_of(index * 128, 128)
        q, k, v = (qkv_ref[:, pl.ds(part * D + at, 128)] for part in range(3))
        d_attn = dattn_ref[:, pl.ds(at, 128)]
        dq, dk, dv = [None, None], [None, None], [None, None]
        for head in range(2):
            mine = low if head == 0 else jnp.logical_not(low)
            q_mine, k_mine, v_mine, d_mine = (jnp.where(mine, t, zero) for t in (q, k, v, d_attn))
            for block in range(2):
                count, rows = half * (block + 1), slice(block * half, (block + 1) * half)
                probs = probs_ref[2 * index + head, rows, :count]
                d_probs = nt(d_mine[rows], v_mine[:count])
                wide = probs.astype(F32)
                weighted = wide * d_probs
                delta = jnp.sum(weighted, 1, keepdims=True)
                d_scores = (weighted - wide * delta).astype(BF)
                add(dq, block, nn(d_scores, k_mine[:count]))
                for other in range(block + 1):
                    keys = slice(other * half, (other + 1) * half)
                    add(dk, other, tn(d_scores[:, keys], q_mine[rows]))
                    add(dv, other, tn(probs[:, keys], d_mine[rows]))
        for block in range(2):
            rows = slice(block * half, (block + 1) * half)
            d_qkv[rows, pl.ds(at, 128)] = (dq[block] * 0.125).astype(BF)
            d_qkv[rows, pl.ds(D + at, 128)] = (dk[block] * 0.125).astype(BF)
            d_qkv[rows, pl.ds(2 * D + at, 128)] = dv[block].astype(BF)
        return carry

    lax.fori_loop(0, 6, pair, 0)
    for part in range(3):
        cols = slice(part * D, (part + 1) * D)
        grads_ref[:, cols] = tn(h1p_ref[...], d_qkv[:, cols]).astype(BF)
    turn = hot(iota((D, D), 0) == nat_ref[...])
    d_h1 = nt(nt(d_qkv[...], w_ref[...]).astype(BF), turn)
    x_hat, scale = norm(tok_ref[...].astype(F32))
    d_in, d_gain, d_bias = norm_back(d_h1, x_hat, scale, vec_ref[0:1])
    gx_ref[...] = dxm_ref[...] + d_in
    sub = iota((128, D), 0)
    rows = jnp.where(sub == 16, d_gain, 0.0) + jnp.where(sub == 18, d_bias, 0.0)
    grads_ref[:, 3 * D :] = tn(turn, jnp.transpose(rows).astype(BF)).astype(BF)


def back_two(nat, d_attn, probs, qkv, h1p, d_x_mid, tokens, vec, w):
    vmem = pl.BlockSpec(memory_space=pltpu.VMEM)
    return pl.pallas_call(
        back_two_body,
        grid=(1,),
        in_specs=[vmem] * 8 + [pl.BlockSpec((D, 3 * D), lambda i: (0, 0))],
        out_specs=[vmem] * 2,
        out_shape=[like(ROW, D, dtype=F32), like(D, 3 * D + 128)],
        scratch_shapes=[pltpu.VMEM((ROW, 3 * D), BF)],
        compiler_params=pltpu.CompilerParams(vmem_limit_bytes=56 * MIB),
        cost_estimate=cost(2 * 512 * 768 * 9000, 22 * 10**6),
    )(nat, d_attn, probs, qkv, h1p, d_x_mid, tokens, vec, w)


def merge_body(sid_ref, ret_ref, gate_ref, xmid_ref, out_ref):
    s0, s1 = sid_ref[:, 0:1], sid_ref[:, 1:2]
    y0 = y1 = jnp.zeros((ROW, D), F32)
    for part in range(4):
        slot = iota((ROW, 4 * CAP), 1) + part * 4 * CAP
        values = ret_ref[part * 4 * CAP : (part + 1) * 4 * CAP, :]
        y0 = y0 + nn(hot(slot == s0), values)
        y1 = y1 + nn(hot(slot == s1), values)
    out_ref[...] = (xmid_ref[...] + (gate_ref[:, 0:1] * y0 + gate_ref[:, 1:2] * y1)).astype(BF)


def merge(sid, returned, gate, x_mid):
    return pl.pallas_call(
        merge_body,
        out_shape=like(ROW, D),
        compiler_params=pltpu.CompilerParams(vmem_limit_bytes=40 * MIB),
        cost_estimate=cost(4 * 512 * 1536 * 768, 6 * 10**6),
    )(sid, returned, gate, x_mid)


def shift(value, axis, by):
    count = lax.axis_size(axis)
    return lax.ppermute(value, axis, [(i, (i + by) % count) for i in range(count)])


def ordered(mine, other, index):
    first = jnp.where(index == 0, mine, other)
    second = jnp.where(index == 0, other, mine)
    return first, second


FAR = ("x", "yh", "yl")
PEERS = ("c", "z", "yl")


def to_all(rows, names):
    return lax.all_to_all(rows, names, split_axis=0, concat_axis=0, tiled=True)


def gather_dense(block):
    width = block.shape[1]
    near = to_all(jnp.broadcast_to(block[None], (16, 8, width)), FAR)
    rows = near[:, :6].reshape(96, width)
    return near, rows


def spread(rows):
    pieces = []
    parts = [rows] + [shift(rows, "z", step) for step in (1, 2, 3)]
    for part in parts:
        pieces += [part, shift(part, "c", 1)]
    return pieces


def natural_rows():
    c, z = lax.axis_index("c"), lax.axis_index("z")
    step, other, i = (jnp.arange(768) // 192, (jnp.arange(768) // 96) % 2, jnp.arange(768) % 96)
    core, deep = (c + other) % 2, (z - step) % 4
    return (((i // 12) * 2 + core) * 48 + (deep * 2 + (i // 6) % 2) * 6 + i % 6).astype(jnp.int32)


def scatter_dense(grads):
    width = grads.shape[1]
    parts = grads.reshape(4, 2, 96, width)
    sums = [
        parts[step, 0].astype(F32) + shift(parts[step, 1], "c", 1).astype(F32) for step in range(4)
    ]
    total = sums[0]
    for step in (1, 2, 3):
        total = total + shift(sums[step].astype(BF), "z", -step).astype(F32)
    blocks = jnp.pad(total.astype(BF).reshape(16, 6, width), ((0, 0), (0, 2), (0, 0)))
    return jnp.sum(to_all(blocks, FAR).astype(F32), 0)[:6]


def at(value, index, axis):
    return lax.dynamic_index_in_dim(value, index, axis, False)


def halves(grad):
    parts = grad.reshape(8, 2, grad.shape[0] // 16, grad.shape[1])
    got = lax.ppermute(parts[:, 1], "c", [(0, 1)])
    mine = jnp.where(lax.axis_index("c") == 0, parts[:, 0], got)
    return mine.reshape(4, 2, *mine.shape[1:])


def over_x(mine):
    x = lax.axis_index("x")
    total = at(mine, x, 0).astype(F32)
    for step in (1, 3, 2):
        total = total + shift(at(mine, (x + step) % 4, 0), "x", step).astype(F32)
    return total


def over_y(mine, axis):
    y = lax.axis_index("yh")
    return at(mine, y, axis).astype(F32) + shift(at(mine, 1 - y, axis).astype(BF), "yh", 1).astype(F32)


def shards(
    tokens,
    seq_lengths,
    key_mask,
    routes,
    cotangent,
    qkv_weight,
    out_weight,
    router_weight,
    norm_gains,
    norm_biases,
    up_train,
    down_train,
    up_frozen,
    down_frozen,
):
    core = lax.axis_index("c")

    small = jnp.concatenate((router_weight, norm_gains.T, norm_biases.T), 1)
    block = jnp.concatenate((qkv_weight, out_weight, jnp.pad(small, ((0, 0), (0, 108)))), 1)
    near, rows = gather_dense(jnp.pad(block.astype(BF), ((0, 2), (0, 0))))
    nat = natural_rows().reshape(1, D)

    g_slots, sid, sidt = route(routes, cotangent)
    g_slots, near = lax.optimization_barrier((g_slots, near))
    g_rows = to_all(g_slots.reshape(16, CAP, D), PEERS)

    up_t, down_t = up_train[0].astype(BF), down_train[0].astype(BF)
    up_f, down_f = up_frozen[0], down_frozen[0]
    up_other = shift(jnp.where(core == 0, up_f, up_t), "c", 1)
    down_other = shift(jnp.where(core == 0, down_f, down_t), "c", 1)
    up_two = jnp.concatenate(ordered(jnp.where(core == 0, up_t, up_f), up_other, core), 0)
    down_two = jnp.concatenate(ordered(jnp.where(core == 0, down_t, down_f), down_other, core), 0)
    w_up = lax.all_gather(up_two, ("x", "yh"), tiled=True)
    w_down = lax.all_gather(down_two, ("x", "yh"), tiled=True)

    pieces = spread(rows)
    pieces, g_rows = lax.optimization_barrier((pieces, g_rows))
    w, h1p, qkv, probs, attnp, x_mid, h2, gate, vec, router, sent = forward(
        seq_lengths[0], nat, key_mask.reshape(1, ROW), tokens, sid, sidt, pieces
    )

    arrived = to_all(sent.reshape(16, LINE, D), PEERS)
    out, back, x_rows, d_out, act, d_up = experts(arrived, g_rows, w_up, w_down)
    d_back = to_all(back, PEERS)
    grad_down_l = tn(act, d_out).astype(BF)
    grad_up_l = tn(x_rows, d_up).astype(BF)
    down_mine = halves(grad_down_l)
    up_mine = halves(grad_up_l)
    grad_down = over_x(over_y(down_mine, 1).astype(BF))[None]
    grad_up = over_y(over_x(up_mine), 0)[None]

    out, d_back = lax.optimization_barrier((out, d_back))
    returned = to_all(out, PEERS)
    d_x_mid, d_attn, grads_one = back_one(
        nat, sid, d_back.reshape(16 * LINE, D), gate, router, vec, cotangent, x_mid, h2, attnp, w
    )
    own_one = scatter_dense(grads_one)
    input_grad, grads_two = back_two(nat, d_attn, probs, qkv, h1p, d_x_mid, tokens, vec, w)
    own_two = scatter_dense(grads_two)
    block_out = merge(sid, returned.reshape(16 * CAP, D), gate, x_mid)
    small = own_one[:, D:] + own_two[:, 3 * D :]
    return (
        block_out,
        input_grad,
        own_two[:, : 3 * D],
        own_one[:, :D],
        small[:, :16],
        small[:, 16:18].T,
        small[:, 18:20].T,
        grad_up,
        grad_down,
    )


def solution(mesh):
    fine = Mesh(mesh.devices.reshape(SIZES), NAMES)
    by_row = P(NAMES, None)
    by_column = P(None, NAMES)
    by_expert = P(NARROW, WIDE, None)
    return jax.shard_map(
        shards,
        mesh=fine,
        in_specs=(by_row, by_row, P(NAMES)) + (by_row,) * 5 + (by_column,) * 2 + (by_expert,) * 4,
        out_specs=(by_row,) * 5 + (by_column,) * 2 + (by_expert,) * 2,
        check_vma=False,
    )
```

time: 529 us -> 478 us (0.904)
  matrix products: 147 us -> 21.1 us
  Pallas kernels: 0 us -> 104 us
  waiting for transfers between devices: 216 us -> 158 us
  blocking collectives: 0 us -> 50.3 us
  other arithmetic: 56 us -> 21.9 us
  starting transfers between devices: 52.7 us -> 75.6 us
  local copies, waits for them, and re-layouts: 36.2 us -> 25.3 us
    dot_general x27 -> x2, matrix products: 147 us -> 21.1 us  [tn(): lax.dot_general(a, b, (((0,), (0,)), ((), ())), preferred_element_type=F32)]
    pallas_call x0 -> x6, Pallas kernels: none -> 104 us  [the longest x1 38.1 us: experts(): pl.pallas_call(expert_body, grid=(16 // SOURCES,), in_specs=[by_source(LI...]
    all_to_all x6, waiting for transfers between devices: 134 us -> 42 us  [to_all(): return lax.all_to_all(rows, names, split_axis=0, concat_axis=0, tiled=True)]
    all_to_all x0 -> x1, blocking collectives: none -> 50.3 us  [to_all(): return lax.all_to_all(rows, names, split_axis=0, concat_axis=0, tiled=True)]
    ppermute x15 -> x31, waiting for transfers between devices: 58.8 us -> 89.7 us  [shift(): lax.ppermute(value, axis, [(i, (i + by) % count) for i in range(count)])]
    all_gather x1, waiting for transfers between devices: 0.01 us -> 26.4 us  [shards(): w_down = lax.all_gather(down_two, ('x', 'yh'), tiled=True)]
    reduce_scatter x2 -> x0, waiting for transfers between devices: 23.3 us -> none  [expert_grad(): lax.psum_scatter(mine, ('x', 'yh'), scatter_dimension=0, tiled=True)]
    ppermute x15 -> x31, starting transfers between devices: 16.1 us -> 34.5 us  [shift(): lax.ppermute(value, axis, [(i, (i + by) % count) for i in range(count)])]
  transfers between devices with their start and end apart: 27 -> 41, of which waited for: 14 -> 17; matrix products, arithmetic and copies ran while one was open for 36% -> 10% of each run, Pallas kernels for 0% -> 13%
where the time goes in v2:
time: 478 us; the launch traced here: 471 us
  waiting for transfers between devices  158 us (33%)
  Pallas kernels  104 us (22%)
  starting transfers between devices  75.6 us (16%)
  blocking collectives  50.3 us (11%)
  local copies, waits for them, and re-layouts  25.3 us (5%)
  other arithmetic  21.9 us (5%)
  matrix products  21.1 us (4%)
  between operations  15 us (3%)
    ppermute x31, waiting for transfers between devices, shift(): lax.ppermute(value, axis, [(i, (i + by) % count) for i in range(count)])  89.7 us
    all_to_all x1, blocking collectives, to_all(): return lax.all_to_all(rows, names, split_axis=0, concat_axis=0, tiled=True)  50.3 us
    all_to_all x6, waiting for transfers between devices, to_all(): return lax.all_to_all(rows, names, split_axis=0, concat_axis=0, tiled=True)  42 us
    pallas_call x1, Pallas kernels, experts(): pl.pallas_call(expert_body, grid=(16 // SOURCES,), in_specs=[by_source(LI...  38.1 us
    ppermute x31, starting transfers between devices, shift(): lax.ppermute(value, axis, [(i, (i + by) % count) for i in range(count)])  34.5 us
    all_to_all x6, starting transfers between devices, to_all(): return lax.all_to_all(rows, names, split_axis=0, concat_axis=0, tiled=True)  34 us
    all_gather x1, waiting for transfers between devices, shards(): w_down = lax.all_gather(down_two, ('x', 'yh'), tiled=True)  26.4 us
    pallas_call x1, Pallas kernels, back_two(): pl.pallas_call(back_two_body, grid=(1,), in_specs=[vmem] * 8 + [pl.BlockS...  24.1 us
  transfers between devices with their start and end apart: 41, of which 17 were waited for; matrix products, arithmetic and copies ran while one was open for 10% of the time, Pallas kernels for 13%

profile of v2, /device:TPU:0, one launch (start us, length us, event | category | flops | bytes accessed | tf_op | source)
XLA Modules:
  0.0 471.5 jit_solution(9001476709811845196)
XLA Ops:
  16.4 7.1 %all-to-all-start = ((bf16[16,8,3200]{2,1,0:T(8,128)(2,1)}), bf16[16,8,3200]{2,1,0:T(8,128)(2,1)S(1)}, u32[]{:S(2)}, u32[]{:S(2)}) async-start(bf16[16,8,3200]{2,1,0:T(8,128)(2,1)} %broadcast_in_dim.12), calls=%async_computation | async-start | bytes 1638400 | tf_op jit(solution)/shard_map/all_to_all | solution.py:448
  23.7 4.1 shard_map.205
  29.0 13.4 %all-to-all-done = bf16[16,8,3200]{2,1,0:T(8,128)(2,1)S(1)} async-done(((bf16[16,8,3200]{2,1,0:T(8,128)(2,1)}), bf16[16,8,3200]{2,1,0:T(8,128)(2,1)S(1)}, u32[]{:S(2)}, u32[]{:S(2)}) %all-to-all-start) | async-done | bytes 819232 | tf_op jit(solution)/shard_map/all_to_all | solution.py:448
  42.4 6.1 %all-to-all-start.1 = ((bf16[16,96,768]{2,1,0:T(8,128)(2,1)}), bf16[16,96,768]{2,1,0:T(8,128)(2,1)}, u32[]{:S(2)}, u32[]{:S(2)}) async-start(bf16[16,96,768]{2,1,0:T(8,128)(2,1)} %bitcast.4), calls=%async_computation.1 | async-start | bytes 4718592 | tf_op jit(solution)/shard_map/all_to_all | solution.py:448
  54.9 36.5 %collective-permute-done.1.refs_8_ = bf16[96,3200]{1,0:T(8,128)(2,1)S(1)} collective-permute-done((bf16[96,3200]{1,0:T(8,128)(2,1)S(1)}, bf16[96,3200]{1,0:T(8,128)(2,1)S(1)}, u32[]{:S(2)}, u32[]{:S(2)}) %collective-permute-start.1) | collective-permute-done | bytes 614432 | tf_op jit(solution)/shard_map/ppermute | solution.py:434
  91.4 13.5 %collective-permute-done.3.refs_10_ = bf16[96,3200]{1,0:T(8,128)(2,1)S(1)} collective-permute-done((bf16[96,3200]{1,0:T(8,128)(2,1)S(1)}, bf16[96,3200]{1,0:T(8,128)(2,1)S(1)}, u32[]{:S(2)}, u32[]{:S(2)}) %collective-permute-start.3) | collective-permute-done | bytes 614432 | tf_op jit(solution)/shard_map/ppermute | solution.py:434
  108.1 20.7 %shard_map.206 = (bf16[768,3072]{1,0:T(8,128)(2,1)}, bf16[512,768]{1,0:T(8,128)(2,1)}, bf16[512,2304]{1,0:T(8,128)(2,1)}, bf16[12,512,512]{2,1,0:T(8,128)(2,1)},...) custom-call(s32[2]{0:T(128)} %bitcast.162, ...), custom_call_target="tpu_custom_call" | custom-call | flops 4718592000 | bytes 20000000 | tf_op jit(solution)/shard_map/pallas_call | solution.py:202
  128.9 50.3 %all_to_all.35.sent_ref = bf16[16,112,768]{2,1,0:T(8,128)(2,1)} all-to-all(bf16[16,112,768]{2,1,0:T(8,128)(2,1)} %bitcast.159), channel_id=1, replica_groups=mesh['x'=4,'yh'=2,'c'=2,'z'=4,'yl'=2] {'c','z','yl'}, dimensions={0} | all-to-all | bytes 5505024 | tf_op jit(solution)/shard_map/all_to_all | solution.py:448
  179.2 26.4 %all-gather.5.cloned.1.call-done.down_ref = bf16[3072,768]{1,0:T(8,128)(2,1)} async-done(((bf16[384,768]{1,0:T(8,128)(2,1)}), bf16[3072,768]{1,0:T(8,128)(2,1)}) %all-gather.5.cloned.1.call-update) | async-done | bytes 4718608 | tf_op jit(solution)/shard_map/all_gather | solution.py:544
  205.6 38.1 %shard_map.207 = (bf16[16,96,768]{2,1,0:T(8,128)(2,1)}, bf16[16,112,768]{2,1,0:T(8,128)(2,1)}, bf16[1536,768]{1,0:T(8,128)(2,1)}, bf16[1536,768]{1,0:T(8,128)(2,...) custom-call(bf16[16,112,768]{2,1,0:T(8,128)(2,1)} %all_to_all.35.sent_ref, ...), custom_call_target="tpu_custom_call" | custom-call | flops 28991029248 | bytes 40000000 | tf_op jit(solution)/shard_map/pallas_call | solution.py:268
  243.7 10.9 %convolution_convert_fusion.1 = bf16[768,3072]{1,0:T(8,128)(2,1)S(1)} fusion(bf16[1536,768]{1,0:T(8,128)(2,1)} %get-tuple-element.79, bf16[1536,3072]{1,0:T(8,128)(2,1)} %get-tuple-element.80), kind=kOutput, calls=%fused_computation.1 | convolution fusion | flops 7250116608 | bytes 16515072 | tf_op jit(solution)/shard_map/dot_general | solution.py:35
  260.5 4.9 %all-to-all-start.3 = ((bf16[16,112,768]{2,1,0:T(8,128)(2,1)}), bf16[16,112,768]{2,1,0:T(8,128)(2,1)}, u32[]{:S(2)}, u32[]{:S(2)}) async-start(bf16[16,112,768]{2,1,0:T(8,128)(2,1)} %get-tuple-element.61), calls=%async_computation.3 | async-start | bytes 5505024 | tf_op jit(solution)/shard_map/all_to_all | solution.py:448
  265.5 10.2 %convolution_convert_fusion = bf16[3072,768]{1,0:T(8,128)(2,1)S(1)} fusion(bf16[1536,3072]{1,0:T(8,128)(2,1)} %get-tuple-element.81, bf16[1536,768]{1,0:T(8,128)(2,1)S(1)} %copy-done.30), kind=kOutput, calls=%fused_computation | convolution fusion | flops 7250116608 | bytes 16515072 | tf_op jit(solution)/shard_map/dot_general | solution.py:35
  279.5 4.1 collective-permute-start.28
  285.2 15.2 %all-to-all-done.3 = bf16[16,112,768]{2,1,0:T(8,128)(2,1)} async-done(((bf16[16,112,768]{2,1,0:T(8,128)(2,1)}), bf16[16,112,768]{2,1,0:T(8,128)(2,1)}, u32[]{:S(2)}, u32[]{:S(2)}) %all-to-all-start.3) | async-done | bytes 2752544 | tf_op jit(solution)/shard_map/all_to_all | solution.py:448
  300.5 12.7 %shard_map.209 = (f32[512,768]{1,0:T(8,128)}, bf16[512,768]{1,0:T(8,128)(2,1)S(1)}, bf16[768,896]{1,0:T(8,128)(2,1)S(1)}) custom-call(s32[1,768]{1,0:T(1,128)S(1)} %copy-done, s32[512,128]{1,0:T(8,128)S(1)} %copy-done.7, bf16[1792,768]{1,0:T(8,128)(2,1)} %bitcast.11.dback_ref, f32[512,128]{1,0:T(8,128)S(1)} %copy-done.8, bf16[768,128]{1,0:T(8,128)(2,1)S(1)} %copy-done.9, ...), custom_call_target="tpu_custom_call" | custom-call | flops 3381657600 | bytes 12000000 | tf_op jit(solution)/shard_map/pallas_call | solution.py:334
  315.0 24.1 %shard_map.210 = (f32[512,768]{1,0:T(8,128)}, bf16[768,2432]{1,0:T(8,128)(2,1)}) custom-call(s32[1,768]{1,0:T(1,128)} %fusion.34.refs_1_.nat_ref, bf16[512,768]{1,0:T(8,128)(2,1)} %copy-done.5, bf16[12,512,512]{2,1,0:T(8,128)(2,1)} %get-tuple-element.72.probs_ref, bf16[512,2304]{1,0:T(8,128)(2,1)} %get-tuple-element.73.qkv_ref, ...), custom_call_target="tpu_custom_call" | custom-call | flops 7077888000 | bytes 22000000 | tf_op jit(solution)/shard_map/pallas_call | solution.py:400
  356.3 4.1 collective-permute-start.15
  386.0 7.1 %all-to-all-done.6 = bf16[16,8,896]{2,1,0:T(8,128)(2,1)S(1)} async-done(((bf16[16,8,896]{2,1,0:T(8,128)(2,1)}), bf16[16,8,896]{2,1,0:T(8,128)(2,1)S(1)}, u32[]{:S(2)}, u32[]{:S(2)}) %all-to-all-start.6) | async-done | bytes 229408 | tf_op jit(solution)/shard_map/all_to_all | solution.py:448
  393.1 4.6 all-to-all-start.5
  402.1 6.3 %all-to-all-done.5 = bf16[16,8,2432]{2,1,0:T(8,128)(2,1)} async-done(((bf16[16,8,2432]{2,1,0:T(8,128)(2,1)}), bf16[16,8,2432]{2,1,0:T(8,128)(2,1)}, u32[]{:S(2)}, u32[]{:S(2)}) %all-to-all-start.5) | async-done | bytes 622624 | tf_op jit(solution)/shard_map/all_to_all | solution.py:448
  408.4 7.4 %all-to-all-start.4 = ((bf16[16,96,768]{2,1,0:T(8,128)(2,1)}), bf16[16,96,768]{2,1,0:T(8,128)(2,1)S(1)}, u32[]{:S(2)}, u32[]{:S(2)}) async-start(bf16[16,96,768]{2,1,0:T(8,128)(2,1)} %get-tuple-element.62), calls=%async_computation.4 | async-start | bytes 4718592 | tf_op jit(solution)/shard_map/all_to_all | solution.py:448
  427.0 26.4 %collective-permute-done.27 = bf16[48,3072]{1,0:T(8,128)(2,1)S(1)} collective-permute-done((bf16[48,3072]{1,0:T(8,128)(2,1)S(1)}, bf16[48,3072]{1,0:T(8,128)(2,1)S(1)}, u32[]{:S(2)}, u32[]{:S(2)}) %collective-permute-start.27) | collective-permute-done | bytes 294944 | tf_op jit(solution)/shard_map/ppermute | solution.py:434
  459.8 4.4 shard_map.208
  (180 shorter events, 97.9 us)
Async XLA Ops:
  7.2 172.0 %all-gather.3.cloned.1.call-start = ((), (), s32[]{:S(2)}) async-start(), calls=%async_computation.7 | async-start | bytes 5308416 | tf_op jit(solution)/shard_map/all_gather | solution.py:543
  12.3 193.3 %all-gather.5.cloned.1.call-start = ((), (), s32[]{:S(2)}) async-start(), calls=%async_computation.8 | async-start | bytes 5308416 | tf_op jit(solution)/shard_map/all_gather | solution.py:544
  16.4 26.0 %all-to-all-start = ((bf16[16,8,3200]{2,1,0:T(8,128)(2,1)}), bf16[16,8,3200]{2,1,0:T(8,128)(2,1)S(1)}, u32[]{:S(2)}, u32[]{:S(2)}) async-start(bf16[16,8,3200]{2,1,0:T(8,128)(2,1)} %broadcast_in_dim.12), calls=%async_computation | async-start | bytes 1638400 | tf_op jit(solution)/shard_map/all_to_all | solution.py:448
  42.4 65.7 %all-to-all-start.1 = ((bf16[16,96,768]{2,1,0:T(8,128)(2,1)}), bf16[16,96,768]{2,1,0:T(8,128)(2,1)}, u32[]{:S(2)}, u32[]{:S(2)}) async-start(bf16[16,96,768]{2,1,0:T(8,128)(2,1)} %bitcast.4), calls=%async_computation.1 | async-start | bytes 4718592 | tf_op jit(solution)/shard_map/all_to_all | solution.py:448
  48.8 42.6 %collective-permute-start.1 = (bf16[96,3200]{1,0:T(8,128)(2,1)S(1)}, bf16[96,3200]{1,0:T(8,128)(2,1)S(1)}, u32[]{:S(2)}, u32[]{:S(2)}) collective-permute-start(bf16[96,3200]{1,0:T(8,128)(2,1)S(1)} %reshape.384.refs_6_), channel_id=1, source_target_pairs={{0,2},{2,4},{4,6},{6,0},{1,3},{3,5},{5,7},{7,1},{8,10},{10,12},{12... | collective-permute-start | bytes 1843208 | tf_op jit(solution)/shard_map/ppermute | solution.py:434
  50.7 54.1 %collective-permute-start.3 = (bf16[96,3200]{1,0:T(8,128)(2,1)S(1)}, bf16[96,3200]{1,0:T(8,128)(2,1)S(1)}, u32[]{:S(2)}, u32[]{:S(2)}) collective-permute-start(bf16[96,3200]{1,0:T(8,128)(2,1)S(1)} %reshape.384.refs_6_), channel_id=1, source_target_pairs={{0,4},{2,6},{4,0},{6,2},{1,5},{3,7},{5,1},{7,3},{8,12},{10,14},{12... | collective-permute-start | bytes 1843208 | tf_op jit(solution)/shard_map/ppermute | solution.py:434
  53.4 51.5 %collective-permute-start.5 = (bf16[96,3200]{1,0:T(8,128)(2,1)S(1)}, bf16[96,3200]{1,0:T(8,128)(2,1)}, u32[]{:S(2)}, u32[]{:S(2)}) collective-permute-start(bf16[96,3200]{1,0:T(8,128)(2,1)S(1)} %reshape.384.refs_6_), channel_id=1, source_target_pairs={{0,6},{2,0},{4,2},{6,4},{1,7},{3,1},{5,3},{7,5},{8,14},{10,8},{12,... | collective-permute-start | bytes 1843208 | tf_op jit(solution)/shard_map/ppermute | solution.py:434
  54.9 51.4 %collective-permute-start = (bf16[96,3200]{1,0:T(8,128)(2,1)S(1)}, bf16[96,3200]{1,0:T(8,128)(2,1)}, u32[]{:S(2)}, u32[]{:S(2)}) collective-permute-start(bf16[96,3200]{1,0:T(8,128)(2,1)S(1)} %reshape.384.refs_6_), channel_id=1, source_target_pairs={{0,8},{8,0},{1,9},{9,1},{2,10},{10,2},{3,11},{11,3},{4,12},{12,4},... | collective-permute-start | bytes 1843208 | tf_op jit(solution)/shard_map/ppermute | solution.py:434
  257.6 26.0 %collective-permute-start.23 = (bf16[8,48,3072]{2,1,0:T(8,128)(2,1)}, bf16[8,48,3072]{2,1,0:T(8,128)(2,1)}, u32[]{:S(2)}, u32[]{:S(2)}) collective-permute-start(bf16[8,48,3072]{2,1,0:T(8,128)(2,1)} %slice_bitcast_fusion.2), channel_id=1, source_target_pairs={{0,8},{1,9},{2,10},{3,11},{4,12},{5,13},{6,14},{7,15},{16,24},{17,... | collective-permute-start | bytes 7077896 | tf_op jit(solution)/shard_map/ppermute | solution.py:492
  260.5 39.9 %all-to-all-start.3 = ((bf16[16,112,768]{2,1,0:T(8,128)(2,1)}), bf16[16,112,768]{2,1,0:T(8,128)(2,1)}, u32[]{:S(2)}, u32[]{:S(2)}) async-start(bf16[16,112,768]{2,1,0:T(8,128)(2,1)} %get-tuple-element.61), calls=%async_computation.3 | async-start | bytes 5505024 | tf_op jit(solution)/shard_map/all_to_all | solution.py:448
  279.5 62.4 %collective-permute-start.28 = (bf16[8,192,768]{2,1,0:T(8,128)(2,1)}, bf16[8,192,768]{2,1,0:T(8,128)(2,1)}, u32[]{:S(2)}, u32[]{:S(2)}) collective-permute-start(bf16[8,192,768]{2,1,0:T(8,128)(2,1)} %slice_bitcast_fusion), channel_id=1, source_target_pairs={{0,8},{1,9},{2,10},{3,11},{4,12},{5,13},{6,14},{7,15},{16,24},{17,... | collective-permute-start | bytes 7077896 | tf_op jit(solution)/shard_map/ppermute | solution.py:492
  314.1 27.9 %collective-permute-start.17 = (bf16[96,896]{1,0:T(8,128)(2,1)S(1)}, bf16[96,896]{1,0:T(8,128)(2,1)S(1)}, u32[]{:S(2)}, u32[]{:S(2)}) collective-permute-start(bf16[96,896]{1,0:T(8,128)(2,1)S(1)} %get-tuple-element.123), channel_id=1, source_target_pairs={{0,8},{8,0},{1,9},{9,1},{2,10},{10,2},{3,11},{11,3},{4,12},{12,4},... | collective-permute-start | bytes 516104 | tf_op jit(solution)/shard_map/ppermute | solution.py:434
  314.2 30.1 %collective-permute-start.19 = (bf16[96,896]{1,0:T(8,128)(2,1)S(1)}, bf16[96,896]{1,0:T(8,128)(2,1)S(1)}, u32[]{:S(2)}, u32[]{:S(2)}) collective-permute-start(bf16[96,896]{1,0:T(8,128)(2,1)S(1)} %get-tuple-element.122), channel_id=1, source_target_pairs={{0,8},{8,0},{1,9},{9,1},{2,10},{10,2},{3,11},{11,3},{4,12},{12,4},... | collective-permute-start | bytes 516104 | tf_op jit(solution)/shard_map/ppermute | solution.py:434
  314.7 30.5 %collective-permute-start.21 = (bf16[96,896]{1,0:T(8,128)(2,1)S(1)}, bf16[96,896]{1,0:T(8,128)(2,1)S(1)}, u32[]{:S(2)}, u32[]{:S(2)}) collective-permute-start(bf16[96,896]{1,0:T(8,128)(2,1)S(1)} %get-tuple-element.121), channel_id=1, source_target_pairs={{0,8},{8,0},{1,9},{9,1},{2,10},{10,2},{3,11},{11,3},{4,12},{12,4},... | collective-permute-start | bytes 516104 | tf_op jit(solution)/shard_map/ppermute | solution.py:434
  345.2 24.4 %collective-permute-start.9 = (bf16[96,2432]{1,0:T(8,128)(2,1)}, bf16[96,2432]{1,0:T(8,128)(2,1)}, u32[]{:S(2)}, u32[]{:S(2)}) collective-permute-start(bf16[96,2432]{1,0:T(8,128)(2,1)} %get-tuple-element.110), channel_id=1, source_target_pairs={{0,8},{8,0},{1,9},{9,1},{2,10},{10,2},{3,11},{11,3},{4,12},{12,4},... | collective-permute-start | bytes 1400840 | tf_op jit(solution)/shard_map/ppermute | solution.py:434
  352.6 23.0 %collective-permute-start.11 = (bf16[96,2432]{1,0:T(8,128)(2,1)}, bf16[96,2432]{1,0:T(8,128)(2,1)}, u32[]{:S(2)}, u32[]{:S(2)}) collective-permute-start(bf16[96,2432]{1,0:T(8,128)(2,1)} %get-tuple-element.114), channel_id=1, source_target_pairs={{0,6},{2,0},{4,2},{6,4},{1,7},{3,1},{5,3},{7,5},{8,14},{10,8},{12,... | collective-permute-start | bytes 1400840 | tf_op jit(solution)/shard_map/ppermute | solution.py:434
  362.8 58.0 %collective-permute-start.29 = (bf16[4,192,768]{2,1,0:T(8,128)(2,1)}, bf16[4,192,768]{2,1,0:T(8,128)(2,1)}, u32[]{:S(2)}, u32[]{:S(2)}) collective-permute-start(bf16[4,192,768]{2,1,0:T(8,128)(2,1)} %dynamic-slice_bitcast_fusion), channel_id=1, source_target_pairs={{0,16},{16,0},{1,17},{17,1},{2,18},{18,2},{3,19},{19,3},{4,20},{20... | collective-permute-start | bytes 3538952 | tf_op jit(solution)/shard_map/ppermute | solution.py:434
  365.7 27.3 %all-to-all-start.6 = ((bf16[16,8,896]{2,1,0:T(8,128)(2,1)}), bf16[16,8,896]{2,1,0:T(8,128)(2,1)S(1)}, u32[]{:S(2)}, u32[]{:S(2)}) async-start(bf16[16,8,896]{2,1,0:T(8,128)(2,1)} %pad.20), calls=%async_computation.6 | async-start | bytes 458752 | tf_op jit(solution)/shard_map/all_to_all | solution.py:448
  369.6 28.1 %collective-permute-start.24 = (bf16[2,48,3072]{2,1,0:T(8,128)(2,1)}, bf16[2,48,3072]{2,1,0:T(8,128)(2,1)}, u32[]{:S(2)}, u32[]{:S(2)}) collective-permute-start(bf16[2,48,3072]{2,1,0:T(8,128)(2,1)} %get-tuple-element.117), channel_id=1, source_target_pairs={{0,32},{32,64},{64,96},{96,0},{1,33},{33,65},{65,97},{97,1},{2,34}... | collective-permute-start | bytes 1769480 | tf_op jit(solution)/shard_map/ppermute | solution.py:434
  408.4 50.0 %all-to-all-start.4 = ((bf16[16,96,768]{2,1,0:T(8,128)(2,1)}), bf16[16,96,768]{2,1,0:T(8,128)(2,1)S(1)}, u32[]{:S(2)}, u32[]{:S(2)}) async-start(bf16[16,96,768]{2,1,0:T(8,128)(2,1)} %get-tuple-element.62), calls=%async_computation.4 | async-start | bytes 4718592 | tf_op jit(solution)/shard_map/all_to_all | solution.py:448
  416.9 36.4 %collective-permute-start.27 = (bf16[48,3072]{1,0:T(8,128)(2,1)S(1)}, bf16[48,3072]{1,0:T(8,128)(2,1)S(1)}, u32[]{:S(2)}, u32[]{:S(2)}) collective-permute-start(bf16[48,3072]{1,0:T(8,128)(2,1)S(1)} %fusion.23), channel_id=1, source_target_pairs={{0,16},{16,0},{1,17},{17,1},{2,18},{18,2},{3,19},{19,3},{4,20},{20... | collective-permute-start | bytes 884744 | tf_op jit(solution)/shard_map/ppermute | solution.py:434
  422.8 31.4 %collective-permute-start.30 = (bf16[192,768]{1,0:T(8,128)(2,1)S(1)}, bf16[192,768]{1,0:T(8,128)(2,1)S(1)}, u32[]{:S(2)}, u32[]{:S(2)}) collective-permute-start(bf16[192,768]{1,0:T(8,128)(2,1)S(1)} %get-tuple-element.127), channel_id=1, source_target_pairs={{0,32},{32,64},{64,96},{96,0},{1,33},{33,65},{65,97},{97,1},{2,34}... | collective-permute-start | bytes 884744 | tf_op jit(solution)/shard_map/ppermute | solution.py:434
  423.8 30.5 %collective-permute-start.31 = (bf16[192,768]{1,0:T(8,128)(2,1)S(1)}, bf16[192,768]{1,0:T(8,128)(2,1)S(1)}, u32[]{:S(2)}, u32[]{:S(2)}) collective-permute-start(bf16[192,768]{1,0:T(8,128)(2,1)S(1)} %get-tuple-element.129), channel_id=1, source_target_pairs={{0,96},{32,0},{64,32},{96,64},{1,97},{33,1},{65,33},{97,65},{2,98}... | collective-permute-start | bytes 884744 | tf_op jit(solution)/shard_map/ppermute | solution.py:434
  426.1 28.1 %collective-permute-start.32 = (bf16[192,768]{1,0:T(8,128)(2,1)S(1)}, bf16[192,768]{1,0:T(8,128)(2,1)S(1)}, u32[]{:S(2)}, u32[]{:S(2)}) collective-permute-start(bf16[192,768]{1,0:T(8,128)(2,1)S(1)} %get-tuple-element.128), channel_id=1, source_target_pairs={{0,64},{32,96},{64,0},{96,32},{1,65},{33,97},{65,1},{97,33},{2,66}... | collective-permute-start | bytes 884744 | tf_op jit(solution)/shard_map/ppermute | solution.py:434
  (48 other events, 546.9 us)
Sparse Core Ops, SparseCore 0:
  12.3 101.4 all-gather.2
  116.7 88.8 all-gather.4

commit v3 on v2

--- a/solution.py
+++ b/solution.py
@@ -21,6 +21,7 @@
 GELU_ONE = 0.7978845608028654
 GELU_CUBE = GELU_ONE * 0.044715
 MIB = 1024 * 1024
+SMALL = pl.CostEstimate(flops=10**6, bytes_accessed=10**4, transcendentals=0)
 
 
 def nn(a, b):
@@ -45,10 +46,6 @@
 
 def like(*dims, dtype=BF):
     return jax.ShapeDtypeStruct(dims, dtype)
-
-
-def cost(flops, moved, transcendentals=0):
-    return pl.CostEstimate(flops=flops, bytes_accessed=moved, transcendentals=transcendentals)
 
 
 def tail_of(line):
@@ -108,7 +105,7 @@
         route_body,
         out_shape=[like(16 * CAP, D), like(ROW, 128, dtype=jnp.int32), like(8, ROW, dtype=jnp.int32)],
         compiler_params=pltpu.CompilerParams(vmem_limit_bytes=32 * MIB),
-        cost_estimate=cost(2 * 1536 * 512 * 768, 4 * 10**6),
+        cost_estimate=SMALL,
     )(routes, cotangent)
 
 
@@ -221,19 +218,43 @@
             pltpu.VMEM((ROW, ROW), F32),
         ],
         compiler_params=pltpu.CompilerParams(vmem_limit_bytes=56 * MIB),
-        cost_estimate=cost(2 * 512 * 768 * 6000, 20 * 10**6, 12 * 512 * 512),
+        cost_estimate=SMALL,
     )(lens, nat, mask, tokens, sid, sidt, *pieces)
 
 
 def expert_body(
-    sent_ref, g_ref, up_ref, down_ref, out_ref, back_ref, x_ref, dout_ref, act_ref, dup_ref
+    place_ref, sent_ref, g_ref, up_mine, up_other, down_mine, *refs
 ):
+    down_other = refs[:4]
+    out_ref, back_ref, x_ref, dout_ref, act_ref, dup_ref, up_ref, down_ref, sems = refs[4:]
+    x_place, y_place = place_ref[0], place_ref[1]
+
+    def loads():
+        for i in range(4):
+            mine, other = 2 * i + y_place, 2 * i + 1 - y_place
+            far = 2 * lax.rem(x_place - i + 4, 4) + 1 - y_place
+            yield up_mine.at[pl.ds(i * 96, 96), :], up_ref.at[pl.ds(mine * 96, 96), :]
+            yield up_other.at[pl.ds(i * 96, 96), :], up_ref.at[pl.ds(other * 96, 96), :]
+            yield down_mine.at[pl.ds(i * 384, 384), :], down_ref.at[pl.ds(mine * 384, 384), :]
+            yield down_other[i], down_ref.at[pl.ds(far * 384, 384), :]
+
+    @pl.when(pl.program_id(0) == 0)
+    def _():
+        copies = [
+            pltpu.make_async_copy(source, target, sems.at[i])
+            for i, (source, target) in enumerate(loads())
+        ]
+        for copy in copies:
+            copy.start()
+        for copy in copies:
+            copy.wait()
+
     for s in range(SOURCES):
-        rows = slice(s * CAP, (s + 1) * CAP)
-        x_ref[rows, :] = sent_ref[s, :CAP, :]
+        first, last = s * CAP, (s + 1) * CAP
+        x_ref[first:last, :] = sent_ref[s, :CAP, :]
         gate = line_of(sent_ref[s, CAP:LINE, :])
         column = jnp.transpose(jnp.broadcast_to(gate, (128, 128)))[:CAP, :1]
-        dout_ref[rows, :] = (g_ref[s].astype(F32) * column).astype(BF)
+        dout_ref[first:last, :] = (g_ref[s].astype(F32) * column).astype(BF)
     x, d_out = x_ref[...], dout_ref[...]
     for part in range(FF // 256):
         cols = slice(part * 256, (part + 1) * 256)
@@ -254,26 +275,25 @@
             back_ref[s, :CAP, cols] = back[s * CAP : (s + 1) * CAP]
     for s in range(SOURCES):
         d_gate = jnp.sum(out_ref[s].astype(F32) * g_ref[s].astype(F32), -1, keepdims=True)
-        wide = jnp.concatenate(
-            [jnp.broadcast_to(d_gate, (CAP, 128)), jnp.zeros((128 - CAP, 128), F32)], 0
-        )
+        d_gate = jnp.broadcast_to(d_gate, (CAP, 128))
+        wide = jnp.concatenate([d_gate, jnp.zeros((128 - CAP, 128), F32)], 0)
         back_ref[s, CAP:LINE, :] = tail_of(jnp.transpose(wide)[0:1])
 
 
-def experts(sent, g, w_up, w_down):
+def experts(place, sent, g, up_mine, up_other, down_mine, down_other):
     rows = SOURCES * CAP
-    once = pl.Buffered(1)
+    anywhere = pl.BlockSpec(memory_space=pl.ANY)
     by_source = lambda size: pl.BlockSpec((SOURCES, size, D), lambda i: (i, 0, 0))
     by_rows = lambda width: pl.BlockSpec((rows, width), lambda i: (i, 0))
     return pl.pallas_call(
         expert_body,
         grid=(16 // SOURCES,),
         in_specs=[
+            pl.BlockSpec(memory_space=pltpu.SMEM),
             by_source(LINE),
             by_source(CAP),
-            pl.BlockSpec((D, FF), lambda i: (0, 0), pipeline_mode=once),
-            pl.BlockSpec((FF, D), lambda i: (0, 0), pipeline_mode=once),
-        ],
+        ]
+        + [anywhere] * 7,
         out_specs=[
             by_source(CAP), by_source(LINE), by_rows(D), by_rows(D), by_rows(FF), by_rows(FF),
         ],
@@ -285,14 +305,53 @@
             like(16 * CAP, FF),
             like(16 * CAP, FF),
         ],
+        scratch_shapes=[
+            pltpu.VMEM((D, FF), BF),
+            pltpu.VMEM((FF, D), BF),
+            pltpu.SemaphoreType.DMA((16,)),
+        ],
         compiler_params=pltpu.CompilerParams(vmem_limit_bytes=60 * MIB),
-        cost_estimate=cost(8 * 1536 * 768 * 3072, 40 * 10**6, 1536 * 3072),
-    )(sent, g, w_up, w_down)
+        cost_estimate=SMALL,
+    )(place, sent, g, up_mine, up_other, down_mine, *down_other)
+
+
+def weight_body(x_ref, dout_ref, act_ref, dup_ref, up0_ref, up1_ref, down0_ref, down1_ref):
+    up = tn(x_ref[...], dup_ref[...]).astype(BF)
+    for block in range(8):
+        rows = slice(block * 48, (block + 1) * 48)
+        up0_ref[rows, :] = up[block * 96 : block * 96 + 48]
+        up1_ref[rows, :] = up[block * 96 + 48 : (block + 1) * 96]
+    down = tn(act_ref[...], dout_ref[...]).astype(BF)
+    down0_ref[...] = down[:192]
+    down1_ref[...] = down[192:]
+
+
+def weights(x, d_out, act, d_up):
+    whole = pl.BlockSpec((16 * CAP, D), lambda i: (0, 0))
+    columns = pl.BlockSpec((16 * CAP, 384), lambda i: (0, i))
+    up = pl.BlockSpec((384, 384), lambda i: (0, i))
+    down = pl.BlockSpec((192, D), lambda i: (i, 0))
+    return pl.pallas_call(
+        weight_body,
+        grid=(8,),
+        in_specs=[whole, whole, columns, columns],
+        out_specs=[up, up, down, down],
+        out_shape=[like(384, FF), like(384, FF), like(1536, D), like(1536, D)],
+        compiler_params=pltpu.CompilerParams(vmem_limit_bytes=48 * MIB),
+        cost_estimate=SMALL,
+    )(x, d_out, act, d_up)
+
+
+def put_rows(keep_ref, away_ref, cols, values):
+    for step in range(4):
+        rows = slice(step * 96, (step + 1) * 96)
+        keep_ref[rows, cols] = values[step * 192 : step * 192 + 96]
+        away_ref[rows, cols] = values[step * 192 + 96 : (step + 1) * 192]
 
 
 def back_one_body(
     nat_ref, sid_ref, dback_ref, gate_ref, router_ref, vec_ref, cot_ref, xmid_ref, h2_ref,
-    attnp_ref, w_ref, dxm_ref, dattn_ref, grads_ref,
+    attnp_ref, w_ref, dxm_ref, dattn_ref, keep_ref, away_ref,
 ):
     lane = iota((ROW, 128), 1)
     s0, s1, w0, w1, r0, r1 = (sid_ref[:, at : at + 1] for at in range(6))
@@ -321,12 +380,12 @@
     d_proj = d_x_mid.astype(BF)
     turn = hot(iota((D, D), 0) == nat_ref[...])
     dattn_ref[...] = nt(nt(d_proj, w_ref[...]).astype(BF), turn).astype(BF)
-    grads_ref[:, :D] = tn(attnp_ref[...], d_proj).astype(BF)
+    put_rows(keep_ref, away_ref, slice(0, D), tn(attnp_ref[...], d_proj).astype(BF))
     d_router = tn(h2_ref[...], high) + tn(h2_ref[...], low)
     sub = iota((128, D), 0)
     rows = jnp.where(sub == 17, d_gain, 0.0) + jnp.where(sub == 19, d_bias, 0.0)
     small = d_router + jnp.transpose(rows)
-    grads_ref[:, D:] = tn(turn, small.astype(BF)).astype(BF)
+    put_rows(keep_ref, away_ref, slice(D, D + 128), tn(turn, small.astype(BF)).astype(BF))
 
 
 def back_one(nat, sid, d_back, gate, router, vec, cotangent, x_mid, h2, attnp, w):
@@ -335,17 +394,14 @@
         back_one_body,
         grid=(1,),
         in_specs=[vmem] * 10 + [pl.BlockSpec((D, D), lambda i: (0, 3))],
-        out_specs=[vmem] * 3,
-        out_shape=[like(ROW, D, dtype=F32), like(ROW, D), like(D, D + 128)],
+        out_specs=[vmem] * 4,
+        out_shape=[like(ROW, D, dtype=F32), like(ROW, D), like(384, D + 128), like(384, D + 128)],
         compiler_params=pltpu.CompilerParams(vmem_limit_bytes=48 * MIB),
-        cost_estimate=cost(2 * 512 * 768 * 4300, 12 * 10**6),
+        cost_estimate=SMALL,
     )(nat, sid, d_back, gate, router, vec, cotangent, x_mid, h2, attnp, w)
 
 
-def back_two_body(
-    nat_ref, dattn_ref, probs_ref, qkv_ref, h1p_ref, dxm_ref, tok_ref, vec_ref, w_ref,
-    gx_ref, grads_ref, d_qkv,
-):
+def attention_back(base, dattn_ref, probs_ref, qkv_ref, d_qkv):
     low = iota((1, 128), 1) < 64
     zero = jnp.zeros((), BF)
     half = ROW // 2
@@ -354,7 +410,8 @@
         terms[at] = term if terms[at] is None else terms[at] + term
 
     def pair(index, carry):
-        at = pl.multiple_of(index * 128, 128)
+        at = pl.multiple_of((base + index) * 128, 128)
+        to = pl.multiple_of(index * 128, 128)
         q, k, v = (qkv_ref[:, pl.ds(part * D + at, 128)] for part in range(3))
         d_attn = dattn_ref[:, pl.ds(at, 128)]
         dq, dk, dv = [None, None], [None, None], [None, None]
@@ -376,37 +433,83 @@
                     add(dv, other, tn(probs[:, keys], d_mine[rows]))
         for block in range(2):
             rows = slice(block * half, (block + 1) * half)
-            d_qkv[rows, pl.ds(at, 128)] = (dq[block] * 0.125).astype(BF)
-            d_qkv[rows, pl.ds(D + at, 128)] = (dk[block] * 0.125).astype(BF)
-            d_qkv[rows, pl.ds(2 * D + at, 128)] = dv[block].astype(BF)
+            d_qkv[rows, pl.ds(to, 128)] = (dq[block] * 0.125).astype(BF)
+            d_qkv[rows, pl.ds(384 + to, 128)] = (dk[block] * 0.125).astype(BF)
+            d_qkv[rows, pl.ds(768 + to, 128)] = dv[block].astype(BF)
         return carry
 
-    lax.fori_loop(0, 6, pair, 0)
+    lax.fori_loop(0, 3, pair, 0)
+
+
+def back_two_body(dattn_ref, probs_ref, qkv_ref, h1p_ref, dqkv_ref, keep_ref, away_ref):
+    attention_back(0, dattn_ref, probs_ref, qkv_ref, dqkv_ref)
     for part in range(3):
-        cols = slice(part * D, (part + 1) * D)
-        grads_ref[:, cols] = tn(h1p_ref[...], d_qkv[:, cols]).astype(BF)
+        cols = slice(part * 384, (part + 1) * 384)
+        put_rows(keep_ref, away_ref, cols, tn(h1p_ref[...], dqkv_ref[:, cols]).astype(BF))
+
+
+def back_two(d_attn, probs, qkv, h1p):
+    vmem = pl.BlockSpec(memory_space=pltpu.VMEM)
+    return pl.pallas_call(
+        back_two_body,
+        grid=(1,),
+        in_specs=[vmem, pl.BlockSpec((6, ROW, ROW), lambda i: (0, 0, 0)), vmem, vmem],
+        out_specs=[vmem] * 3,
+        out_shape=[like(ROW, 1152), like(384, 1152), like(384, 1152)],
+        compiler_params=pltpu.CompilerParams(vmem_limit_bytes=40 * MIB),
+        cost_estimate=SMALL,
+    )(d_attn, probs, qkv, h1p)
+
+
+def back_three_body(dattn_ref, probs_ref, qkv_ref, dqkv_ref):
+    attention_back(3, dattn_ref, probs_ref, qkv_ref, dqkv_ref)
+
+
+def back_three(d_attn, probs, qkv):
+    vmem = pl.BlockSpec(memory_space=pltpu.VMEM)
+    return pl.pallas_call(
+        back_three_body,
+        grid=(1,),
+        in_specs=[vmem, pl.BlockSpec((6, ROW, ROW), lambda i: (1, 0, 0)), vmem],
+        out_specs=vmem,
+        out_shape=like(ROW, 1152),
+        compiler_params=pltpu.CompilerParams(vmem_limit_bytes=40 * MIB),
+        cost_estimate=SMALL,
+    )(d_attn, probs, qkv)
+
+
+def back_four_body(
+    nat_ref, h1p_ref, first_ref, second_ref, dxm_ref, tok_ref, vec_ref, w_ref,
+    gx_ref, keep_ref, away_ref,
+):
+    d_h1p = jnp.zeros((ROW, D), F32)
+    for part in range(3):
+        cols = slice(part * 384, (part + 1) * 384)
+        d_h1p = d_h1p + nt(first_ref[:, cols], w_ref[:, part * D : part * D + 384])
+        d_h1p = d_h1p + nt(second_ref[:, cols], w_ref[:, part * D + 384 : (part + 1) * D])
+        put_rows(keep_ref, away_ref, cols, tn(h1p_ref[...], second_ref[:, cols]).astype(BF))
     turn = hot(iota((D, D), 0) == nat_ref[...])
-    d_h1 = nt(nt(d_qkv[...], w_ref[...]).astype(BF), turn)
+    d_h1 = nt(d_h1p.astype(BF), turn)
     x_hat, scale = norm(tok_ref[...].astype(F32))
     d_in, d_gain, d_bias = norm_back(d_h1, x_hat, scale, vec_ref[0:1])
     gx_ref[...] = dxm_ref[...] + d_in
     sub = iota((128, D), 0)
     rows = jnp.where(sub == 16, d_gain, 0.0) + jnp.where(sub == 18, d_bias, 0.0)
-    grads_ref[:, 3 * D :] = tn(turn, jnp.transpose(rows).astype(BF)).astype(BF)
-
-
-def back_two(nat, d_attn, probs, qkv, h1p, d_x_mid, tokens, vec, w):
+    small = tn(turn, jnp.transpose(rows).astype(BF)).astype(BF)
+    put_rows(keep_ref, away_ref, slice(1152, 1280), small)
+
+
+def back_four(nat, h1p, first, second, d_x_mid, tokens, vec, w):
     vmem = pl.BlockSpec(memory_space=pltpu.VMEM)
     return pl.pallas_call(
-        back_two_body,
+        back_four_body,
         grid=(1,),
-        in_specs=[vmem] * 8 + [pl.BlockSpec((D, 3 * D), lambda i: (0, 0))],
-        out_specs=[vmem] * 2,
-        out_shape=[like(ROW, D, dtype=F32), like(D, 3 * D + 128)],
-        scratch_shapes=[pltpu.VMEM((ROW, 3 * D), BF)],
-        compiler_params=pltpu.CompilerParams(vmem_limit_bytes=56 * MIB),
-        cost_estimate=cost(2 * 512 * 768 * 9000, 22 * 10**6),
-    )(nat, d_attn, probs, qkv, h1p, d_x_mid, tokens, vec, w)
+        in_specs=[vmem] * 7 + [pl.BlockSpec((D, 3 * D), lambda i: (0, 0))],
+        out_specs=[vmem] * 3,
+        out_shape=[like(ROW, D, dtype=F32), like(384, 1280), like(384, 1280)],
+        compiler_params=pltpu.CompilerParams(vmem_limit_bytes=40 * MIB),
+        cost_estimate=SMALL,
+    )(nat, h1p, first, second, d_x_mid, tokens, vec, w)
 
 
 def merge_body(sid_ref, ret_ref, gate_ref, xmid_ref, out_ref):
@@ -425,8 +528,76 @@
         merge_body,
         out_shape=like(ROW, D),
         compiler_params=pltpu.CompilerParams(vmem_limit_bytes=40 * MIB),
-        cost_estimate=cost(4 * 512 * 1536 * 768, 6 * 10**6),
+        cost_estimate=SMALL,
     )(sid, returned, gate, x_mid)
+
+
+def to_blocks_body(place_ref, *refs):
+    out_ref, total = refs[-2:]
+    x, y = place_ref[0], 2 * place_ref[1] + place_ref[2]
+    col = 0
+    for group in range(3):
+        own, parts = refs[4 * group], refs[4 * group + 1 : 4 * group + 4]
+        width = own.shape[1]
+        value = own[...]
+        for part in parts:
+            value = value + part[...].astype(F32)
+        total[0:96, col : col + width] = value
+        col += width
+    total[96:104, :] = jnp.zeros((8, col), F32)
+    for k in range(16):
+        to = lax.rem(x - k % 4 + 4, 4) * 4 + lax.rem(y - k // 4 + 4, 4)
+        out_ref[to] = total[6 * k : 6 * k + 8, :].astype(BF)
+
+
+def to_blocks(place, parts):
+    vmem = pl.BlockSpec(memory_space=pltpu.VMEM)
+    width = sum(part.shape[1] for part in parts[::4])
+    return pl.pallas_call(
+        to_blocks_body,
+        in_specs=[pl.BlockSpec(memory_space=pltpu.SMEM)] + [vmem] * 12,
+        out_shape=like(16, 8, width),
+        scratch_shapes=[pltpu.VMEM((104, width), F32)],
+        compiler_params=pltpu.CompilerParams(vmem_limit_bytes=24 * MIB),
+        cost_estimate=SMALL,
+    )(place, *parts)
+
+
+def from_blocks_body(in_ref, qkv_ref, out_ref, small_ref):
+    total = in_ref[0].astype(F32)
+    for k in range(1, 16):
+        total = total + in_ref[k].astype(F32)
+    out_ref[...] = total[:6, :D]
+    for part in range(3):
+        at = 896 + part * 384
+        qkv_ref[:, part * D : part * D + 384] = total[:6, at : at + 384]
+        qkv_ref[:, part * D + 384 : (part + 1) * D] = total[:6, at + 1152 : at + 1536]
+    small_ref[...] = total[:6, D : D + 128] + total[:6, 3200:3328]
+
+
+def from_blocks(blocks):
+    return pl.pallas_call(
+        from_blocks_body,
+        out_shape=[like(6, 3 * D, dtype=F32), like(6, D, dtype=F32), like(6, 128, dtype=F32)],
+        compiler_params=pltpu.CompilerParams(vmem_limit_bytes=16 * MIB),
+        cost_estimate=SMALL,
+    )(blocks)
+
+
+def block_body(qkv_ref, out_ref, small_ref, to_ref):
+    to_ref[...] = jnp.zeros(to_ref.shape, BF)
+    to_ref[0:6, : 3 * D] = qkv_ref[...].astype(BF)
+    to_ref[0:6, 3 * D : FF] = out_ref[...].astype(BF)
+    to_ref[0:6, FF : FF + 20] = small_ref[...].astype(BF)
+
+
+def block_of(qkv, out, small):
+    return pl.pallas_call(
+        block_body,
+        out_shape=like(8, FF + 128),
+        compiler_params=pltpu.CompilerParams(vmem_limit_bytes=16 * MIB),
+        cost_estimate=SMALL,
+    )(qkv, out, small)
 
 
 def shift(value, axis, by):
@@ -448,50 +619,42 @@
     return lax.all_to_all(rows, names, split_axis=0, concat_axis=0, tiled=True)
 
 
-def gather_dense(block):
-    width = block.shape[1]
-    near = to_all(jnp.broadcast_to(block[None], (16, 8, width)), FAR)
-    rows = near[:, :6].reshape(96, width)
-    return near, rows
-
-
-def spread(rows):
-    pieces = []
-    parts = [rows] + [shift(rows, "z", step) for step in (1, 2, 3)]
-    for part in parts:
-        pieces += [part, shift(part, "c", 1)]
-    return pieces
+def spread_x(block):
+    return jnp.stack([block] + [shift(block, "x", step) for step in (1, 2, 3)])
+
+
+def spread_y(along_x):
+    near = [along_x] + [shift(along_x, ("yh", "yl"), step) for step in (1, 2, 3)]
+    return jnp.stack(near)[:, :, :6].reshape(96, along_x.shape[2])
 
 
 def natural_rows():
-    c, z = lax.axis_index("c"), lax.axis_index("z")
-    step, other, i = (jnp.arange(768) // 192, (jnp.arange(768) // 96) % 2, jnp.arange(768) % 96)
+    x, c, z = (lax.axis_index(name) for name in ("x", "c", "z"))
+    y = lax.axis_index("yh") * 2 + lax.axis_index("yl")
+    row = jnp.arange(768)
+    step, other, i = row // 192, (row // 96) % 2, row % 96
     core, deep = (c + other) % 2, (z - step) % 4
-    return (((i // 12) * 2 + core) * 48 + (deep * 2 + (i // 6) % 2) * 6 + i % 6).astype(jnp.int32)
-
-
-def scatter_dense(grads):
-    width = grads.shape[1]
-    parts = grads.reshape(4, 2, 96, width)
-    sums = [
-        parts[step, 0].astype(F32) + shift(parts[step, 1], "c", 1).astype(F32) for step in range(4)
-    ]
-    total = sums[0]
-    for step in (1, 2, 3):
-        total = total + shift(sums[step].astype(BF), "z", -step).astype(F32)
-    blocks = jnp.pad(total.astype(BF).reshape(16, 6, width), ((0, 0), (0, 2), (0, 0)))
-    return jnp.sum(to_all(blocks, FAR).astype(F32), 0)[:6]
+    high, long = (y - i // 24) % 4, (x - (i // 6) % 4) % 4
+    device = ((long * 2 + high // 2) * 2 + core) * 8 + deep * 2 + high % 2
+    return (device * 6 + i % 6).astype(jnp.int32)
+
+
+def over_core(keep, away):
+    return (keep.astype(F32) + shift(away, "c", 1).astype(F32)).reshape(4, 96, keep.shape[1])
+
+
+def along_z(sums):
+    return [sums[0]] + [shift(sums[step].astype(BF), "z", -step) for step in (1, 2, 3)]
 
 
 def at(value, index, axis):
     return lax.dynamic_index_in_dim(value, index, axis, False)
 
 
-def halves(grad):
-    parts = grad.reshape(8, 2, grad.shape[0] // 16, grad.shape[1])
-    got = lax.ppermute(parts[:, 1], "c", [(0, 1)])
-    mine = jnp.where(lax.axis_index("c") == 0, parts[:, 0], got)
-    return mine.reshape(4, 2, *mine.shape[1:])
+def halves(kept, sent):
+    got = lax.ppermute(sent, "c", [(0, 1)])
+    mine = jnp.where(lax.axis_index("c") == 0, kept, got)
+    return mine.reshape(4, 2, mine.shape[0] // 8, mine.shape[1])
 
 
 def over_x(mine):
@@ -525,55 +688,85 @@
 ):
     core = lax.axis_index("c")
 
+    place = jnp.stack([lax.axis_index(name) for name in ("x", "yh", "yl")]).astype(jnp.int32)
+
     small = jnp.concatenate((router_weight, norm_gains.T, norm_biases.T), 1)
-    block = jnp.concatenate((qkv_weight, out_weight, jnp.pad(small, ((0, 0), (0, 108)))), 1)
-    near, rows = gather_dense(jnp.pad(block.astype(BF), ((0, 2), (0, 0))))
+    block = block_of(qkv_weight, out_weight, small)
+    block, routes, up_train, down_train, up_frozen, down_frozen = lax.optimization_barrier(
+        (block, routes, up_train, down_train, up_frozen, down_frozen)
+    )
+    rows = spread_y(spread_x(block))
     nat = natural_rows().reshape(1, D)
-
     g_slots, sid, sidt = route(routes, cotangent)
-    g_slots, near = lax.optimization_barrier((g_slots, near))
+
+    up_t, down_t = up_train[0].astype(BF), down_train[0].astype(BF)
+
+    def for_core(trained, frozen):
+        other = shift(jnp.where(core == 0, frozen, trained), "c", 1)
+        return jnp.concatenate(ordered(jnp.where(core == 0, trained, frozen), other, core), 0)
+
+    up_two, down_two = for_core(up_t, up_frozen[0]), for_core(down_t, down_frozen[0])
+    up_mine = lax.all_gather(up_two, "x", tiled=True)
+    down_mine = lax.all_gather(down_two, "x", tiled=True)
+
+    rows, g_slots, up_two, down_two = lax.optimization_barrier((rows, g_slots, up_two, down_two))
+    parts = [rows] + [shift(rows, "z", step) for step in (1, 2, 3)]
+    up_far, down_far = shift(up_two, "yh", 1), shift(down_two, "yh", 1)
+    parts, up_far, down_far, g_slots = lax.optimization_barrier((parts, up_far, down_far, g_slots))
+    pieces = []
+    for part in parts:
+        pieces += [part, shift(part, "c", 1)]
+    up_other = lax.all_gather(up_far, "x", tiled=True)
+    down_other = [down_far] + [shift(down_far, "x", step) for step in (1, 2, 3)]
+
     g_rows = to_all(g_slots.reshape(16, CAP, D), PEERS)
-
-    up_t, down_t = up_train[0].astype(BF), down_train[0].astype(BF)
-    up_f, down_f = up_frozen[0], down_frozen[0]
-    up_other = shift(jnp.where(core == 0, up_f, up_t), "c", 1)
-    down_other = shift(jnp.where(core == 0, down_f, down_t), "c", 1)
-    up_two = jnp.concatenate(ordered(jnp.where(core == 0, up_t, up_f), up_other, core), 0)
-    down_two = jnp.concatenate(ordered(jnp.where(core == 0, down_t, down_f), down_other, core), 0)
-    w_up = lax.all_gather(up_two, ("x", "yh"), tiled=True)
-    w_down = lax.all_gather(down_two, ("x", "yh"), tiled=True)
-
-    pieces = spread(rows)
-    pieces, g_rows = lax.optimization_barrier((pieces, g_rows))
     w, h1p, qkv, probs, attnp, x_mid, h2, gate, vec, router, sent = forward(
         seq_lengths[0], nat, key_mask.reshape(1, ROW), tokens, sid, sidt, pieces
     )
+    sent, g_rows = lax.optimization_barrier((sent, g_rows))
 
     arrived = to_all(sent.reshape(16, LINE, D), PEERS)
-    out, back, x_rows, d_out, act, d_up = experts(arrived, g_rows, w_up, w_down)
+    out, back, x_rows, d_out, act, d_up = experts(
+        place, arrived, g_rows, up_mine, up_other, down_mine, down_other
+    )
     d_back = to_all(back, PEERS)
-    grad_down_l = tn(act, d_out).astype(BF)
-    grad_up_l = tn(x_rows, d_up).astype(BF)
-    down_mine = halves(grad_down_l)
-    up_mine = halves(grad_up_l)
-    grad_down = over_x(over_y(down_mine, 1).astype(BF))[None]
-    grad_up = over_y(over_x(up_mine), 0)[None]
-
-    out, d_back = lax.optimization_barrier((out, d_back))
+    grads = weights(x_rows, d_out, act, d_up)
+    d_back, out, grads = lax.optimization_barrier((d_back, out, grads))
+
     returned = to_all(out, PEERS)
-    d_x_mid, d_attn, grads_one = back_one(
+    down_all = halves(grads[2], grads[3])
+    up_all = halves(grads[0], grads[1])
+    d_x_mid, d_attn, keep, away = back_one(
         nat, sid, d_back.reshape(16 * LINE, D), gate, router, vec, cotangent, x_mid, h2, attnp, w
     )
-    own_one = scatter_dense(grads_one)
-    input_grad, grads_two = back_two(nat, d_attn, probs, qkv, h1p, d_x_mid, tokens, vec, w)
-    own_two = scatter_dense(grads_two)
+    d_attn, down_all, up_all = lax.optimization_barrier((d_attn, down_all, up_all))
+    down_half = over_y(down_all, 1).astype(BF)
+    up_half = over_x(up_all)
+    sums_one = over_core(keep, away)
+    first, keep, away = back_two(d_attn, probs, qkv, h1p)
+    first, sums_one = lax.optimization_barrier((first, sums_one))
+    parts_one = along_z(sums_one)
+    sums_two = over_core(keep, away)
+    second = back_three(d_attn, probs, qkv)
+    second, sums_two, down_half, up_half = lax.optimization_barrier(
+        (second, sums_two, down_half, up_half)
+    )
+    parts_two = along_z(sums_two)
+    grad_down = over_x(down_half)[None]
+    grad_up = over_y(up_half, 0)[None]
+    input_grad, keep, away = back_four(nat, h1p, first, second, d_x_mid, tokens, vec, w)
+    keep, away, returned, parts_one, grad_up, grad_down = lax.optimization_barrier(
+        (keep, away, returned, parts_one, grad_up, grad_down)
+    )
+    parts_three = along_z(over_core(keep, away))
+    blocks = to_all(to_blocks(place, parts_one + parts_two + parts_three), FAR)
+    own_qkv, own_out, small = from_blocks(blocks)
     block_out = merge(sid, returned.reshape(16 * CAP, D), gate, x_mid)
-    small = own_one[:, D:] + own_two[:, 3 * D :]
     return (
         block_out,
         input_grad,
-        own_two[:, : 3 * D],
-        own_one[:, :D],
+        own_qkv,
+        own_out,
         small[:, :16],
         small[:, 16:18].T,
         small[:, 18:20].T,

time: 478 us -> 408 us (0.85)
  blocking collectives: 50.3 us -> 0 us
  waiting for transfers between devices: 158 us -> 129 us
  Pallas kernels: 104 us -> 128 us
  matrix products: 21.1 us -> 0 us
  starting transfers between devices: 75.6 us -> 84 us
    all_to_all x1 -> x0, blocking collectives: 50.3 us -> none  [to_all(): return lax.all_to_all(rows, names, split_axis=0, concat_axis=0, tiled=True)]
    all_gather x2 -> x3, waiting for transfers between devices: 26.4 us -> 0.01 us  [the longest x1 0.01 us: shards(): up_mine = lax.all_gather(up_two, 'x', tiled=True)]
    pallas_call x2 -> x8, Pallas kernels: 62.3 us -> 85.7 us  [the longest x1 40.1 us: experts(): pl.pallas_call(expert_body, grid=(16 // SOURCES,), in_specs=[pl.BlockSpec...]
    dot_general x2 -> x0, matrix products: 21.1 us -> none  [tn(): lax.dot_general(a, b, (((0,), (0,)), ((), ())), preferred_element_type=F32)]
    ppermute x31 -> x40, starting transfers between devices: 34.5 us -> 53.9 us  [shift(): lax.ppermute(value, axis, [(i, (i + by) % count) for i in range(count)])]
    all_to_all x6 -> x5, waiting for transfers between devices: 42 us -> 25.1 us  [to_all(): return lax.all_to_all(rows, names, split_axis=0, concat_axis=0, tiled=True)]
    ppermute x31 -> x40, waiting for transfers between devices: 89.7 us -> 103 us  [shift(): lax.ppermute(value, axis, [(i, (i + by) % count) for i in range(count)])]
    unnamed x65 -> x92, local copies, waits for them, and re-layouts: 8.64 us -> 18.5 us
  transfers between devices with their start and end apart: 41 -> 50, of which waited for: 17 -> 27; matrix products, arithmetic and copies ran while one was open for 10% -> 5% of each run, Pallas kernels for 13% -> 21%
where the time goes in v3:
time: 408 us; the launch traced here: 400 us
  waiting for transfers between devices  129 us (32%)
  Pallas kernels  128 us (31%)
  starting transfers between devices  84 us (21%)
  local copies, waits for them, and re-layouts  23.1 us (6%)
  other arithmetic  21.2 us (5%)
  between operations  14.9 us (4%)
    ppermute x40, waiting for transfers between devices, shift(): lax.ppermute(value, axis, [(i, (i + by) % count) for i in range(count)])  103 us
    ppermute x40, starting transfers between devices, shift(): lax.ppermute(value, axis, [(i, (i + by) % count) for i in range(count)])  53.9 us
    pallas_call x1, Pallas kernels, experts(): pl.pallas_call(expert_body, grid=(16 // SOURCES,), in_specs=[pl.BlockSpec...  40.1 us
    all_to_all x5, waiting for transfers between devices, to_all(): return lax.all_to_all(rows, names, split_axis=0, concat_axis=0, tiled=True)  25.1 us
    all_to_all x5, starting transfers between devices, to_all(): return lax.all_to_all(rows, names, split_axis=0, concat_axis=0, tiled=True)  24.2 us
    pallas_call x1, Pallas kernels, weights(): pl.pallas_call(weight_body, grid=(8,), in_specs=[whole, whole, columns, c...  23.8 us
    pallas_call x1, Pallas kernels, forward(): pl.pallas_call(forward_body, in_specs=[pl.BlockSpec(memory_space=pltpu.SM...  20.7 us
    unnamed x92, local copies, waits for them, and re-layouts  18.5 us
  transfers between devices with their start and end apart: 50, of which 27 were waited for; matrix products, arithmetic and copies ran while one was open for 5% of the time, Pallas kernels for 21%

profile of v3, /device:TPU:0, one launch (start us, length us, event | category | flops | bytes accessed | tf_op | source)
XLA Modules:
  0.0 400.4 jit_solution(18230558127515370761)
XLA Ops:
  51.2 14.3 %collective-permute-done.11 = bf16[96,3072]{1,0:T(8,128)(2,1)} collective-permute-done((bf16[96,3072]{1,0:T(8,128)(2,1)S(1)}, bf16[96,3072]{1,0:T(8,128)(2,1)}, u32[]{:S(2)}, u32[]{:S(2)}) %collective-permute-start.11) | collective-permute-done | bytes 589856 | tf_op jit(solution)/shard_map/ppermute | solution.py:605
  65.5 9.6 %collective-permute-done.12.refs_0_ = bf16[384,768]{1,0:T(8,128)(2,1)} collective-permute-done((bf16[384,768]{1,0:T(8,128)(2,1)S(1)}, bf16[384,768]{1,0:T(8,128)(2,1)}, u32[]{:S(2)}, u32[]{:S(2)}) %collective-permute-start.12) | collective-permute-done | bytes 589856 | tf_op jit(solution)/shard_map/ppermute | solution.py:605
  76.0 4.9 %all-to-all-start = ((bf16[16,96,768]{2,1,0:T(8,128)(2,1)}), bf16[16,96,768]{2,1,0:T(8,128)(2,1)S(1)}, u32[]{:S(2)}, u32[]{:S(2)}) async-start(bf16[16,96,768]{2,1,0:T(8,128)(2,1)} %bitcast.19), calls=%async_computation | async-start | bytes 4718592 | tf_op jit(solution)/shard_map/all_to_all | solution.py:619
  86.7 20.7 %shard_map.207 = (bf16[768,3072]{1,0:T(8,128)(2,1)}, bf16[512,768]{1,0:T(8,128)(2,1)}, bf16[512,2304]{1,0:T(8,128)(2,1)}, bf16[12,512,512]{2,1,0:T(8,128)(2,1)},...) custom-call(s32[2]{0:T(128)} %bitcast.113, ...), custom_call_target="tpu_custom_call" | custom-call | flops 1000000 | bytes 10000 | tf_op jit(solution)/shard_map/pallas_call | solution.py:199
  112.8 4.4 %all-to-all-start.1 = ((bf16[16,112,768]{2,1,0:T(8,128)(2,1)}), bf16[16,112,768]{2,1,0:T(8,128)(2,1)S(1)}, u32[]{:S(2)}, u32[]{:S(2)}) async-start(bf16[16,112,768]{2,1,0:T(8,128)(2,1)} %bitcast.102), calls=%async_computation.1 | async-start | bytes 5505024 | tf_op jit(solution)/shard_map/all_to_all | solution.py:619
  122.4 12.3 %collective-permute-done.17.refs_1_ = bf16[384,768]{1,0:T(8,128)(2,1)} collective-permute-done((bf16[384,768]{1,0:T(8,128)(2,1)}, bf16[384,768]{1,0:T(8,128)(2,1)}, u32[]{:S(2)}, u32[]{:S(2)}) %collective-permute-start.17) | collective-permute-done | bytes 589856 | tf_op jit(solution)/shard_map/ppermute | solution.py:605
  134.7 12.6 %collective-permute-done.18.refs_2_ = bf16[384,768]{1,0:T(8,128)(2,1)} collective-permute-done((bf16[384,768]{1,0:T(8,128)(2,1)}, bf16[384,768]{1,0:T(8,128)(2,1)}, u32[]{:S(2)}, u32[]{:S(2)}) %collective-permute-start.18) | collective-permute-done | bytes 589856 | tf_op jit(solution)/shard_map/ppermute | solution.py:605
  147.7 4.4 %all-to-all-done.1.sent_ref = bf16[16,112,768]{2,1,0:T(8,128)(2,1)S(1)} async-done(((bf16[16,112,768]{2,1,0:T(8,128)(2,1)}), bf16[16,112,768]{2,1,0:T(8,128)(2,1)S(1)}, u32[]{:S(2)}, u32[]{:S(2)}) %all-to-all-start.1) | async-done | bytes 2752544 | tf_op jit(solution)/shard_map/all_to_all | solution.py:619
  153.7 40.1 %shard_map.208 = (bf16[16,96,768]{2,1,0:T(8,128)(2,1)}, bf16[16,112,768]{2,1,0:T(8,128)(2,1)}, bf16[1536,768]{1,0:T(8,128)(2,1)}, bf16[1536,768]{1,0:T(8,128)(2,...) custom-call(s32[3]{0:T(128)} %pad_add_fusion.place_ref, bf16[16,112,768]{2,1,0:T(8,128)(2,1)} %copy-done.26, ...), custom_call_target="tpu_custom_call" | custom-call | flops 1000000 | bytes 10000 | tf_op jit(solution)/shard_map/pallas_call | solution.py:288
  193.8 4.5 %all-to-all-start.2 = ((bf16[16,112,768]{2,1,0:T(8,128)(2,1)}), bf16[16,112,768]{2,1,0:T(8,128)(2,1)}, u32[]{:S(2)}, u32[]{:S(2)}) async-start(bf16[16,112,768]{2,1,0:T(8,128)(2,1)} %get-tuple-element.113), calls=%async_computation.2 | async-start | bytes 5505024 | tf_op jit(solution)/shard_map/all_to_all | solution.py:619
  198.3 23.8 %shard_map.209 = (bf16[384,3072]{1,0:T(8,128)(2,1)S(1)}, bf16[384,3072]{1,0:T(8,128)(2,1)S(1)}, bf16[1536,768]{1,0:T(8,128)(2,1)}, bf16[1536,768]{1,0:T(8,128)(2,1)}) custom-call(bf16[1536,768]{1,0:T(8,128)(2,1)} %get-tuple-element.115.x_ref, bf16[1536,768]{1,0:T(8,128)(2,1)} %get-tuple-element.116.dout_ref, bf16[1536,3072]{1,0:T(8,128)(2,1)} %get-tuple-element.117.act_ref, ...), custom_call_target="tpu_custom_call" | custom-call | flops 1000000 | bytes 10000 | tf_op jit(solution)/shard_map/pallas_call | solution.py:334
  225.0 8.1 %all-to-all-done.2 = bf16[16,112,768]{2,1,0:T(8,128)(2,1)} async-done(((bf16[16,112,768]{2,1,0:T(8,128)(2,1)}), bf16[16,112,768]{2,1,0:T(8,128)(2,1)}, u32[]{:S(2)}, u32[]{:S(2)}) %all-to-all-start.2) | async-done | bytes 2752544 | tf_op jit(solution)/shard_map/all_to_all | solution.py:619
  240.2 13.6 %shard_map.210 = (f32[512,768]{1,0:T(8,128)}, bf16[512,768]{1,0:T(8,128)(2,1)S(1)}, bf16[384,896]{1,0:T(8,128)(2,1)S(1)}, bf16[384,896]{1,0:T(8,128)(2,1)}) custom-call(s32[1,768]{1,0:T(1,128)S(1)} %copy-done.20, s32[512,128]{1,0:T(8,128)S(1)} %copy-done.7, bf16[1792,768]{1,0:T(8,128)(2,1)} %bitcast.21.dback_ref, f32[512,128]{1,0:T(8,128)S(1)} %copy-done.9, ...), custom_call_target="tpu_custom_call" | custom-call | flops 1000000 | bytes 10000 | tf_op jit(solution)/shard_map/pallas_call | solution.py:393
  254.6 4.5 %all-to-all-start.3 = ((bf16[16,96,768]{2,1,0:T(8,128)(2,1)}), bf16[16,96,768]{2,1,0:T(8,128)(2,1)S(1)}, u32[]{:S(2)}, u32[]{:S(2)}) async-start(bf16[16,96,768]{2,1,0:T(8,128)(2,1)} %get-tuple-element.151), calls=%async_computation.3 | async-start | bytes 4718592 | tf_op jit(solution)/shard_map/all_to_all | solution.py:619
  271.6 6.5 %shard_map.211 = (bf16[512,1152]{1,0:T(8,128)(2,1)S(1)}, bf16[384,1152]{1,0:T(8,128)(2,1)S(1)}, bf16[384,1152]{1,0:T(8,128)(2,1)S(1)}) custom-call(bf16[512,768]{1,0:T(8,128)(2,1)S(1)} %get-tuple-element.136.dattn_ref, bf16[12,512,512]{2,1,0:T(8,128)(2,1)S(1)} %bitcast.89, bf16[512,2304]{1,0:T(8,128)(2,1)S(1)} %copy-done, bf16[512,768]{1,0:T(8,128)(2,1)S(1)} %copy-done.2), custom_call_target="tpu_custom_call" | custom-call | flops 1000000 | bytes 10000 | tf_op jit(solution)/shard_map/pallas_call | solution.py:453
  279.5 5.1 %shard_map.212.second_ref = bf16[512,1152]{1,0:T(8,128)(2,1)S(1)} custom-call(bf16[512,768]{1,0:T(8,128)(2,1)S(1)} %get-tuple-element.136.dattn_ref, bf16[12,512,512]{2,1,0:T(8,128)(2,1)S(1)} %bitcast.89, bf16[512,2304]{1,0:T(8,128)(2,1)S(1)} %copy-done), custom_call_target="tpu_custom_call" | custom-call | flops 1000000 | bytes 10000 | tf_op jit(solution)/shard_map/pallas_call | solution.py:470
  299.7 15.7 %collective-permute-done.24 = bf16[4,192,768]{2,1,0:T(8,128)(2,1)} collective-permute-done((bf16[4,192,768]{2,1,0:T(8,128)(2,1)}, bf16[4,192,768]{2,1,0:T(8,128)(2,1)}, u32[]{:S(2)}, u32[]{:S(2)}) %collective-permute-start.24) | collective-permute-done | bytes 1179680 | tf_op jit(solution)/shard_map/ppermute | solution.py:605
  321.5 7.0 %shard_map.213 = (f32[512,768]{1,0:T(8,128)}, bf16[384,1280]{1,0:T(8,128)(2,1)S(1)}, bf16[384,1280]{1,0:T(8,128)(2,1)S(1)}) custom-call(s32[1,768]{1,0:T(1,128)S(1)} %copy-done.20, bf16[512,768]{1,0:T(8,128)(2,1)S(1)} %copy-done.2, bf16[512,1152]{1,0:T(8,128)(2,1)S(1)} %get-tuple-element.142.first_ref, bf16[512,1152]{1,0:T(8,128)(2,1)S(1)} %shard_map.212.second_ref, ...), custom_call_target="tpu_custom_call" | custom-call | flops 1000000 | bytes 10000 | tf_op jit(solution)/shard_map/pallas_call | solution.py:504
  330.5 7.5 %collective-permute-done.34 = bf16[192,768]{1,0:T(8,128)(2,1)S(1)} collective-permute-done((bf16[192,768]{1,0:T(8,128)(2,1)S(1)}, bf16[192,768]{1,0:T(8,128)(2,1)S(1)}, u32[]{:S(2)}, u32[]{:S(2)}) %collective-permute-start.34) | collective-permute-done | bytes 294944 | tf_op jit(solution)/shard_map/ppermute | solution.py:605
  348.4 4.2 %collective-permute-done.35.refs_5_ = bf16[96,1152]{1,0:T(8,128)(2,1)S(1)} collective-permute-done((bf16[96,1152]{1,0:T(8,128)(2,1)S(1)}, bf16[96,1152]{1,0:T(8,128)(2,1)S(1)}, u32[]{:S(2)}, u32[]{:S(2)}) %collective-permute-start.35) | collective-permute-done | bytes 221216 | tf_op jit(solution)/shard_map/ppermute | solution.py:605
  362.3 4.4 %collective-permute-done.41.refs_11_ = bf16[96,1280]{1,0:T(8,128)(2,1)S(1)} collective-permute-done((bf16[96,1280]{1,0:T(8,128)(2,1)S(1)}, bf16[96,1280]{1,0:T(8,128)(2,1)S(1)}, u32[]{:S(2)}, u32[]{:S(2)}) %collective-permute-start.41) | collective-permute-done | bytes 245792 | tf_op jit(solution)/shard_map/ppermute | solution.py:605
  369.2 6.0 %all-to-all-start.4 = ((bf16[16,8,3328]{2,1,0:T(8,128)(2,1)}), bf16[16,8,3328]{2,1,0:T(8,128)(2,1)S(1)}, u32[]{:S(2)}, u32[]{:S(2)}) async-start(bf16[16,8,3328]{2,1,0:T(8,128)(2,1)} %shard_map.215), calls=%async_computation.4 | async-start | bytes 1703936 | tf_op jit(solution)/shard_map/all_to_all | solution.py:619
  377.6 4.4 %shard_map.214 = bf16[512,768]{1,0:T(8,128)(2,1)} custom-call(s32[512,128]{1,0:T(8,128)S(1)} %copy-done.7, bf16[1536,768]{1,0:T(8,128)(2,1)S(1)} %bitcast.92, f32[512,128]{1,0:T(8,128)S(1)} %copy-done.10, f32[512,768]{1,0:T(8,128)S(1)} %copy-done.1), custom_call_target="tpu_custom_call" | custom-call | flops 1000000 | bytes 10000 | tf_op jit(solution)/shard_map/pallas_call | solution.py:527
  382.0 8.5 %all-to-all-done.4.in_ref = bf16[16,8,3328]{2,1,0:T(8,128)(2,1)S(1)} async-done(((bf16[16,8,3328]{2,1,0:T(8,128)(2,1)}), bf16[16,8,3328]{2,1,0:T(8,128)(2,1)S(1)}, u32[]{:S(2)}, u32[]{:S(2)}) %all-to-all-start.4) | async-done | bytes 852000 | tf_op jit(solution)/shard_map/all_to_all | solution.py:619
  (220 shorter events, 138.4 us)
Async XLA Ops:
  7.2 140.5 %all-gather.4.cloned.1.call-start = ((), (), s32[]{:S(2)}) async-start(), calls=%async_computation.5 | async-start | bytes 2949120 | tf_op jit(solution)/shard_map/all_gather | solution.py:709
  16.1 131.6 %all-gather.8.cloned.1.call-start = ((), (), s32[]{:S(2)}) async-start(), calls=%async_computation.7 | async-start | bytes 2949120 | tf_op jit(solution)/shard_map/all_gather | solution.py:710
  41.7 33.5 %collective-permute-start.10 = (bf16[96,3200]{1,0:T(8,128)(2,1)S(1)}, bf16[96,3200]{1,0:T(8,128)(2,1)S(1)}, u32[]{:S(2)}, u32[]{:S(2)}) collective-permute-start(bf16[96,3200]{1,0:T(8,128)(2,1)S(1)} %reshape.510.refs_6_), channel_id=1, source_target_pairs={{0,6},{2,0},{4,2},{6,4},{1,7},{3,1},{5,3},{7,5},{8,14},{10,8},{12,... | collective-permute-start | bytes 1843208 | tf_op jit(solution)/shard_map/ppermute | solution.py:605
  45.8 29.4 %collective-permute-start.8 = (bf16[96,3200]{1,0:T(8,128)(2,1)S(1)}, bf16[96,3200]{1,0:T(8,128)(2,1)}, u32[]{:S(2)}, u32[]{:S(2)}) collective-permute-start(bf16[96,3200]{1,0:T(8,128)(2,1)S(1)} %reshape.510.refs_6_), channel_id=1, source_target_pairs={{0,2},{2,4},{4,6},{6,0},{1,3},{3,5},{5,7},{7,1},{8,10},{10,12},{12... | collective-permute-start | bytes 1843208 | tf_op jit(solution)/shard_map/ppermute | solution.py:605
  45.8 29.4 %collective-permute-start.9 = (bf16[96,3200]{1,0:T(8,128)(2,1)S(1)}, bf16[96,3200]{1,0:T(8,128)(2,1)}, u32[]{:S(2)}, u32[]{:S(2)}) collective-permute-start(bf16[96,3200]{1,0:T(8,128)(2,1)S(1)} %reshape.510.refs_6_), channel_id=1, source_target_pairs={{0,4},{2,6},{4,0},{6,2},{1,5},{3,7},{5,1},{7,3},{8,12},{10,14},{12... | collective-permute-start | bytes 1843208 | tf_op jit(solution)/shard_map/ppermute | solution.py:605
  47.6 17.9 %collective-permute-start.11 = (bf16[96,3072]{1,0:T(8,128)(2,1)S(1)}, bf16[96,3072]{1,0:T(8,128)(2,1)}, u32[]{:S(2)}, u32[]{:S(2)}) collective-permute-start(bf16[96,3072]{1,0:T(8,128)(2,1)S(1)} %copy-done.32), channel_id=1, source_target_pairs={{0,16},{16,0},{1,17},{17,1},{2,18},{18,2},{3,19},{19,3},{4,20},{20... | collective-permute-start | bytes 1769480 | tf_op jit(solution)/shard_map/ppermute | solution.py:605
  50.2 24.9 %collective-permute-start.12 = (bf16[384,768]{1,0:T(8,128)(2,1)S(1)}, bf16[384,768]{1,0:T(8,128)(2,1)}, u32[]{:S(2)}, u32[]{:S(2)}) collective-permute-start(bf16[384,768]{1,0:T(8,128)(2,1)S(1)} %copy-done.33), channel_id=1, source_target_pairs={{0,16},{16,0},{1,17},{17,1},{2,18},{18,2},{3,19},{19,3},{4,20},{20... | collective-permute-start | bytes 1769480 | tf_op jit(solution)/shard_map/ppermute | solution.py:605
  76.0 35.5 %all-to-all-start = ((bf16[16,96,768]{2,1,0:T(8,128)(2,1)}), bf16[16,96,768]{2,1,0:T(8,128)(2,1)S(1)}, u32[]{:S(2)}, u32[]{:S(2)}) async-start(bf16[16,96,768]{2,1,0:T(8,128)(2,1)} %bitcast.19), calls=%async_computation | async-start | bytes 4718592 | tf_op jit(solution)/shard_map/all_to_all | solution.py:619
  80.9 66.8 %all-gather.6.cloned.1.call-start = ((), (), s32[]{:S(2)}) async-start(), calls=%async_computation.6 | async-start | bytes 2949120 | tf_op jit(solution)/shard_map/all_gather | solution.py:719
  112.8 39.2 %all-to-all-start.1 = ((bf16[16,112,768]{2,1,0:T(8,128)(2,1)}), bf16[16,112,768]{2,1,0:T(8,128)(2,1)S(1)}, u32[]{:S(2)}, u32[]{:S(2)}) async-start(bf16[16,112,768]{2,1,0:T(8,128)(2,1)} %bitcast.102), calls=%async_computation.1 | async-start | bytes 5505024 | tf_op jit(solution)/shard_map/all_to_all | solution.py:619
  117.4 29.9 %collective-permute-start.18 = (bf16[384,768]{1,0:T(8,128)(2,1)}, bf16[384,768]{1,0:T(8,128)(2,1)}, u32[]{:S(2)}, u32[]{:S(2)}) collective-permute-start(bf16[384,768]{1,0:T(8,128)(2,1)} %collective-permute-done.12.refs_0_), channel_id=1, source_target_pairs={{0,64},{32,96},{64,0},{96,32},{1,65},{33,97},{65,1},{97,33},{2,66}... | collective-permute-start | bytes 1769480 | tf_op jit(solution)/shard_map/ppermute | solution.py:605
  120.8 26.9 %collective-permute-start.19 = (bf16[384,768]{1,0:T(8,128)(2,1)}, bf16[384,768]{1,0:T(8,128)(2,1)}, u32[]{:S(2)}, u32[]{:S(2)}) collective-permute-start(bf16[384,768]{1,0:T(8,128)(2,1)} %collective-permute-done.12.refs_0_), channel_id=1, source_target_pairs={{0,96},{32,0},{64,32},{96,64},{1,97},{33,1},{65,33},{97,65},{2,98}... | collective-permute-start | bytes 1769480 | tf_op jit(solution)/shard_map/ppermute | solution.py:605
  193.8 39.3 %all-to-all-start.2 = ((bf16[16,112,768]{2,1,0:T(8,128)(2,1)}), bf16[16,112,768]{2,1,0:T(8,128)(2,1)}, u32[]{:S(2)}, u32[]{:S(2)}) async-start(bf16[16,112,768]{2,1,0:T(8,128)(2,1)} %get-tuple-element.113), calls=%async_computation.2 | async-start | bytes 5505024 | tf_op jit(solution)/shard_map/all_to_all | solution.py:619
  233.1 25.9 %collective-permute-start.21 = (bf16[384,3072]{1,0:T(8,128)(2,1)}, bf16[384,3072]{1,0:T(8,128)(2,1)}, u32[]{:S(2)}, u32[]{:S(2)}) collective-permute-start(bf16[384,3072]{1,0:T(8,128)(2,1)} %copy-done.24), channel_id=1, source_target_pairs={{0,8},{1,9},{2,10},{3,11},{4,12},{5,13},{6,14},{7,15},{16,24},{17,... | collective-permute-start | bytes 7077896 | tf_op jit(solution)/shard_map/ppermute | solution.py:655
  236.1 25.1 %collective-permute-start.20 = (bf16[1536,768]{1,0:T(8,128)(2,1)}, bf16[1536,768]{1,0:T(8,128)(2,1)}, u32[]{:S(2)}, u32[]{:S(2)}) collective-permute-start(bf16[1536,768]{1,0:T(8,128)(2,1)} %get-tuple-element.133), channel_id=1, source_target_pairs={{0,8},{1,9},{2,10},{3,11},{4,12},{5,13},{6,14},{7,15},{16,24},{17,... | collective-permute-start | bytes 7077896 | tf_op jit(solution)/shard_map/ppermute | solution.py:655
  254.6 84.4 %all-to-all-start.3 = ((bf16[16,96,768]{2,1,0:T(8,128)(2,1)}), bf16[16,96,768]{2,1,0:T(8,128)(2,1)S(1)}, u32[]{:S(2)}, u32[]{:S(2)}) async-start(bf16[16,96,768]{2,1,0:T(8,128)(2,1)} %get-tuple-element.151), calls=%async_computation.3 | async-start | bytes 4718592 | tf_op jit(solution)/shard_map/all_to_all | solution.py:619
  262.6 22.8 %collective-permute-start.25 = (bf16[2,48,3072]{2,1,0:T(8,128)(2,1)S(1)}, bf16[2,48,3072]{2,1,0:T(8,128)(2,1)S(1)}, u32[]{:S(2)}, u32[]{:S(2)}) collective-permute-start(bf16[2,48,3072]{2,1,0:T(8,128)(2,1)S(1)} %get-tuple-element.187), channel_id=1, source_target_pairs={{0,32},{32,64},{64,96},{96,0},{1,33},{33,65},{65,97},{97,1},{2,34}... | collective-permute-start | bytes 1769480 | tf_op jit(solution)/shard_map/ppermute | solution.py:605
  262.7 28.6 %collective-permute-start.26 = (bf16[2,48,3072]{2,1,0:T(8,128)(2,1)S(1)}, bf16[2,48,3072]{2,1,0:T(8,128)(2,1)S(1)}, u32[]{:S(2)}, u32[]{:S(2)}) collective-permute-start(bf16[2,48,3072]{2,1,0:T(8,128)(2,1)S(1)} %get-tuple-element.189), channel_id=1, source_target_pairs={{0,96},{32,0},{64,32},{96,64},{1,97},{33,1},{65,33},{97,65},{2,98}... | collective-permute-start | bytes 1769480 | tf_op jit(solution)/shard_map/ppermute | solution.py:605
  265.8 29.1 %collective-permute-start.27 = (bf16[2,48,3072]{2,1,0:T(8,128)(2,1)S(1)}, bf16[2,48,3072]{2,1,0:T(8,128)(2,1)}, u32[]{:S(2)}, u32[]{:S(2)}) collective-permute-start(bf16[2,48,3072]{2,1,0:T(8,128)(2,1)S(1)} %get-tuple-element.188), channel_id=1, source_target_pairs={{0,64},{32,96},{64,0},{96,32},{1,65},{33,97},{65,1},{97,33},{2,66}... | collective-permute-start | bytes 1769480 | tf_op jit(solution)/shard_map/ppermute | solution.py:605
  268.5 46.9 %collective-permute-start.24 = (bf16[4,192,768]{2,1,0:T(8,128)(2,1)}, bf16[4,192,768]{2,1,0:T(8,128)(2,1)}, u32[]{:S(2)}, u32[]{:S(2)}) collective-permute-start(bf16[4,192,768]{2,1,0:T(8,128)(2,1)} %dynamic-slice_bitcast_fusion), channel_id=1, source_target_pairs={{0,16},{16,0},{1,17},{17,1},{2,18},{18,2},{3,19},{19,3},{4,20},{20... | collective-permute-start | bytes 3538952 | tf_op jit(solution)/shard_map/ppermute | solution.py:605
  278.1 19.0 %collective-permute-start.23 = (bf16[384,1152]{1,0:T(8,128)(2,1)S(1)}, bf16[384,1152]{1,0:T(8,128)(2,1)}, u32[]{:S(2)}, u32[]{:S(2)}) collective-permute-start(bf16[384,1152]{1,0:T(8,128)(2,1)S(1)} %get-tuple-element.144), channel_id=1, source_target_pairs={{0,8},{8,0},{1,9},{9,1},{2,10},{10,2},{3,11},{11,3},{4,12},{12,4},... | collective-permute-start | bytes 2654216 | tf_op jit(solution)/shard_map/ppermute | solution.py:605
  285.4 53.6 %collective-permute-start.28 = (bf16[96,896]{1,0:T(8,128)(2,1)}, bf16[96,896]{1,0:T(8,128)(2,1)S(1)}, u32[]{:S(2)}, u32[]{:S(2)}) collective-permute-start(bf16[96,896]{1,0:T(8,128)(2,1)} %get-tuple-element.207), channel_id=1, source_target_pairs={{0,6},{2,0},{4,2},{6,4},{1,7},{3,1},{5,3},{7,5},{8,14},{10,8},{12,... | collective-permute-start | bytes 516104 | tf_op jit(solution)/shard_map/ppermute | solution.py:605
  291.2 47.7 %collective-permute-start.29 = (bf16[96,896]{1,0:T(8,128)(2,1)}, bf16[96,896]{1,0:T(8,128)(2,1)S(1)}, u32[]{:S(2)}, u32[]{:S(2)}) collective-permute-start(bf16[96,896]{1,0:T(8,128)(2,1)} %get-tuple-element.206), channel_id=1, source_target_pairs={{0,4},{2,6},{4,0},{6,2},{1,5},{3,7},{5,1},{7,3},{8,12},{10,14},{12... | collective-permute-start | bytes 516104 | tf_op jit(solution)/shard_map/ppermute | solution.py:605
  369.2 21.3 %all-to-all-start.4 = ((bf16[16,8,3328]{2,1,0:T(8,128)(2,1)}), bf16[16,8,3328]{2,1,0:T(8,128)(2,1)S(1)}, u32[]{:S(2)}, u32[]{:S(2)}) async-start(bf16[16,8,3328]{2,1,0:T(8,128)(2,1)} %shard_map.215), calls=%async_computation.4 | async-start | bytes 1703936 | tf_op jit(solution)/shard_map/all_to_all | solution.py:619
  (70 other events, 739.6 us)
Sparse Core Ops, SparseCore 0:
  16.2 35.4 all-gather.3
  53.9 33.0 all-gather.7
  88.7 33.0 all-gather.5
